TPU v7x, 768 devices: a whole 4x8x12 slice. The times are simulated.
768 devices in a mesh: ri: 96 (over z, x, core), ao: 8 (over y).
Axes of the slice: x: 4, y: 8, z: 12, core: 2. Of those that a mesh axis runs over, the one named last changes fastest.
Arguments:
- three_center: bfloat16 [1536, 768, 768], P(('ri', 'ao')), may hold values from -24 to 24
- b_pattern: int32 [1536, 6, 6], P(('ri', 'ao')), may hold values 0 or 1
- density: bfloat16 [768, 768], P('ao')
- d_pattern: int32 [6, 6], replicated, may hold values 0 or 1
Outputs:
- exchange: float32 [768, 768], P('ao', 'ri')
All inputs are finite; a program needn't handle non-finite values. No bound on the sum of `b_pattern` on one device may be relied on, other than what follows from the above.
Results may differ from a plain program's by a relative error of at most 0.0029.
Values may be sent and summed in bfloat16 or wider, within the bound.
No kernel may reach another device: no remote copies, remote signals or barrier semaphores. Data moves between devices by JAX's collectives and lax.ppermute only.
A program may use at most 32 MiB of HBM per device.

v0:
```python
import math

import jax
import jax.numpy as jnp
from jax import lax
from jax.sharding import PartitionSpec as P


def per_device(three_center, b_pattern, density, d_pattern):
    local_rows = three_center.shape[0]
    orbitals = three_center.shape[1]
    block_count = d_pattern.shape[0]
    block_size = orbitals // block_count
    shaped = three_center.reshape(local_rows, block_count, block_size, block_count, block_size)
    keep = b_pattern.reshape(local_rows, block_count, 1, block_count, 1) > 0
    masked_b = jnp.where(keep, shaped, jnp.zeros_like(shaped)).reshape(three_center.shape)
    sym_pattern = jnp.maximum(d_pattern, d_pattern.T).astype(jnp.float32)
    col_block = lax.broadcasted_iota(jnp.int32, (orbitals, block_count), 0) // block_size
    col_onehot = (col_block == lax.broadcasted_iota(jnp.int32, (orbitals, block_count), 1)).astype(
        jnp.float32
    )
    rows_in = lax.all_gather(density, "ao", axis=0, tiled=True)
    row_count = rows_in.shape[0]
    row_block = lax.broadcasted_iota(jnp.int32, (row_count, block_count), 0) // block_size
    row_onehot = (row_block == lax.broadcasted_iota(jnp.int32, (row_count, block_count), 1)).astype(
        jnp.float32
    )
    present = jnp.dot(jnp.dot(row_onehot, sym_pattern), col_onehot.T)
    rows_kept = jnp.where(present > 0, rows_in, jnp.zeros_like(rows_in))
    running = jnp.einsum("pml,ls->pms", masked_b, rows_kept, preferred_element_type=jnp.float32)
    half = running.astype(jnp.bfloat16)
    total_ri = local_rows * lax.axis_size("ri") * lax.axis_size("ao")
    factor_all = jnp.float32(1.0 / math.sqrt(total_ri * orbitals))
    partial_value = (
        jnp.einsum("pms,pns->mn", half, masked_b, preferred_element_type=jnp.float32) * factor_all
    )
    column_part = lax.psum_scatter(partial_value, "ri", scatter_dimension=1, tiled=True)
    owned = lax.psum_scatter(column_part, "ao", scatter_dimension=0, tiled=True)
    return owned


def solution(mesh):
    return jax.shard_map(
        per_device,
        mesh=mesh,
        in_specs=(P(("ri", "ao"), None, None), P(("ri", "ao"), None, None), P("ao", None), P()),
        out_specs=P("ao", "ri"),
        check_vma=False,
    )
```

profile of v0, /device:TPU:1, one launch (start us, length us, event | category | flops | bytes accessed | tf_op | source)
XLA Modules:
  0.0 328.9 jit_solution(17807688955205490956)
XLA Ops:
  6.5 0.0 all-gather.2.cloned.1.call-start
  6.5 0.7 all-gather.2.cloned.1.call-update
  7.3 0.0 reduce-scatter.5.cloned.1.call-start
  7.3 0.7 broadcast_compare_fusion
  8.0 0.8 copy.10
  8.8 0.5 broadcast_in_dim.16
  9.3 0.0 copy-start
  9.3 3.1 broadcast_in_dim.17
  12.4 0.0 copy-start.1
  12.4 0.6 fusion.27
  12.9 44.3 %all-gather.2.cloned.1.call-done = bf16[768,768]{1,0:T(8,128)(2,1)} async-done(((bf16[96,768]{1,0:T(8,128)(2,1)}), bf16[768,768]{1,0:T(8,128)(2,1)}) %all-gather.2.cloned.1.call-update) | async-done | bytes 1179664 | tf_op jit(solution)/shard_map/all_gather | solution.py:22
  57.2 0.0 copy-done
  57.2 4.0 %fusion.11 = bf16[768,768,1]{1,0,2:T(8,128)(2,1)} fusion(bf16[768,768]{1,0:T(8,128)(2,1)} %all-gather.2.cloned.1.call-done, s32[768]{0:T(1024)S(1)} %get-tuple-element.5, s32[768]{0:T(1024)S(1)} %get-tuple-element.6, pred[768]{0:T(1024)(128)(4,1)} %fusion.27, s32[6,6]{1,0:T(8,128)S(1)} %copy-done, s32[6,6]{0,1:T(8,128)S(1)} %copy.10), kind=kOutput, calls=%fused_computation.7 | convolution fusion | flops 8331336 | bytes 2366496 | tf_op jit(solution)/shard_map/dot_general | solution.py:28
  61.2 0.0 copy-done.1
  61.2 7.2 %bitcast_multiply_fusion = f32[768,768]{0,1:T(8,128)} fusion(pred[2,768,768]{2,1,0:T(32,128)(4,1)S(1)} %broadcast_in_dim.17, bf16[2,768,768]{2,1,0:T(8,128)(2,1)S(1)} %copy-done.1, bf16[768,768,1]{1,0,2:T(8,128)(2,1)} %fusion.11), kind=kOutput, calls=%fused_computation | convolution fusion | flops 3628007424 | bytes 7077888 | tf_op jit(solution)/shard_map/pms,pns->mn/dot_general | solution.py:35
  68.4 0.0 reduce-scatter.5.cloned.1.call-update
  68.4 0.0 reduce-scatter.7.cloned.1.call-start
  68.5 206.2 %reduce-scatter.5.cloned.1.call-done = f32[768,8]{0,1:T(8,128)} async-done(((f32[768,768]{0,1:T(8,128)}), f32[768,8]{0,1:T(8,128)}) %reduce-scatter.5.cloned.1.call-update) | async-done | bytes 24592 | tf_op jit(solution)/shard_map/reduce_scatter | solution.py:37
  274.7 1.7 copy.11
  276.3 0.0 reduce-scatter.7.cloned.1.call-update
  276.4 44.6 %reduce-scatter.7.cloned.1.call-done = f32[96,8]{1,0:T(8,128)} async-done(((f32[768,8]{1,0:T(8,128)}), f32[96,8]{1,0:T(8,128)}) %reduce-scatter.7.cloned.1.call-update) | async-done | bytes 3088
  321.0 1.5 copy.12
  (2 shorter events, 0.0 us)
Async XLA Ops:
  6.5 50.7 %all-gather.2.cloned.1.call-start = ((), (), s32[]{:S(2)}) async-start(), calls=%async_computation.2 | async-start | bytes 1327104 | tf_op jit(solution)/shard_map/all_gather | solution.py:22
  7.3 267.4 %reduce-scatter.5.cloned.1.call-start = ((), (), s32[]{:S(2)}) async-start(), calls=%async_computation.3 | async-start | bytes 2383872 | tf_op jit(solution)/shard_map/reduce_scatter | solution.py:37
  9.3 48.0 %copy-start = (s32[6,6]{1,0:T(8,128)S(1)}, s32[6,6]{1,0:T(8,128)}, u32[]{:S(2)}) copy-start(s32[6,6]{1,0:T(8,128)} %param.7) | copy-start | bytes 436
  12.4 48.9 %copy-start.1 = (bf16[2,768,768]{2,1,0:T(8,128)(2,1)S(1)}, bf16[2,768,768]{2,1,0:T(8,128)(2,1)}, u32[]{:S(2)}) copy-start(bf16[2,768,768]{2,1,0:T(8,128)(2,1)} %param.4) | copy-start | bytes 7077892
  68.4 252.5 %reduce-scatter.7.cloned.1.call-start = ((), (), s32[]{:S(2)}) async-start(), calls=%async_computation.4 | async-start | bytes 442368
Sparse Core Ops, SparseCore 0:
  9.7 47.4 all-gather.1
  68.5 206.0 reduce-scatter.4
  277.8 43.1 reduce-scatter.6
where the time goes:
time: 333 us; the launch traced here: 329 us
  waiting for transfers between devices  296 us (89%)
  between operations  13.1 us (4%)
  matrix products  11.2 us (3%)
  local copies, waits for them, and re-layouts  7.46 us (2%)
    reduce_scatter x1, waiting for transfers between devices, per_device(): lax.psum_scatter(partial_value, 'ri', scatter_dimension=1, tiled=True)  206 us
    unnamed x4, waiting for transfers between devices  45.3 us
    all_gather x1, waiting for transfers between devices, per_device(): rows_in = lax.all_gather(density, 'ao', axis=0, tiled=True)  44.3 us
    dot_general x1, matrix products, per_device(): jnp.einsum('pms,pns->mn', half, masked_b, preferred_element_type=jnp.floa...  7.17 us
  transfers between devices with their start and end apart: 3, of which 3 were waited for; matrix products, arithmetic and copies ran while one was open for 2% of the time, Pallas kernels for 0%

commit v1 on v0

v1 whole, which is shorter than its diff:
```python
import functools
import math

import jax
import jax.numpy as jnp
from jax import lax
from jax.experimental import pallas as pl
from jax.experimental.pallas import tpu as pltpu
from jax.sharding import Mesh, PartitionSpec as P

Z, X, C, Y = 12, 4, 2, 8
A, BS, NB = 768, 128, 6
K = 8
G = 16
GROUPS = A // G
ROWS = A // (Y * C)
HALF = A // 2
PACK = ROWS * Z * G // 128
MAIN = 128 // G
VMEM = pl.BlockSpec(memory_space=pltpu.VMEM)
SMEM = pl.BlockSpec(memory_space=pltpu.SMEM)
ANY = pl.BlockSpec(memory_space=pl.ANY)


def place(z, x):
    return (x // 2) * 24 + (z if x % 2 == 0 else 12 + (z + 4) % 12)


def mask_kernel(pattern, b_ref, out_ref):
    p = pl.program_id(0)
    for rb in range(NB):
        for cb in range(NB):
            keep = pattern[p, rb, cb] > 0
            lanes = slice(cb * BS, (cb + 1) * BS)
            for g in range(rb * 8, rb * 8 + 8):
                block = b_ref[0, g, :, lanes]
                out_ref[0, place(g // X, g % X), :, lanes] = jnp.where(keep, block, jnp.zeros_like(block))


def mask_and_order(three_center, b_pattern):
    count = three_center.shape[0]
    spec = pl.BlockSpec((1, GROUPS, G, A), lambda p: (p, 0, 0, 0))
    return pl.pallas_call(
        mask_kernel,
        grid=(count,),
        in_specs=[SMEM, spec],
        out_specs=spec,
        out_shape=jax.ShapeDtypeStruct((count, GROUPS, G, A), jnp.bfloat16),
        name="mask",
    )(b_pattern, three_center.reshape(count, GROUPS, G, A))


def exchange_kernel(count, core_ref, d_pattern, d_own, d_other, b_own, b_other, out_ref, b, d, rows, acc, sems):
    copies = []
    for p in range(2 * count):
        source = b_own.at[p] if p < count else b_other.at[p - count]
        copy = pltpu.make_async_copy(source, b.at[p], sems.at[p])
        copy.start()
        copies.append(copy)
    core = core_ref[0]
    for h, half_ref in ((core, d_own), (1 - core, d_other)):
        for rb in range(NB):
            for cb in range(NB // 2):
                col = h * (NB // 2) + cb
                keep = jnp.maximum(d_pattern[rb, col], d_pattern[col, rb]) > 0
                block = half_ref[rb * BS : (rb + 1) * BS, cb * BS : (cb + 1) * BS]
                lanes = pl.ds(pl.multiple_of(col * BS, BS), BS)
                d[rb * BS : (rb + 1) * BS, lanes] = jnp.where(keep, block, jnp.zeros_like(block))
    acc[...] = jnp.zeros_like(acc)
    for p in range(2 * count):
        copies[p].wait()

        for t in range(Y * ROWS // G):
            per = ROWS // G
            g = (t // per) * (C * per) + core * per + t % per
            z, x = lax.div(g, X), lax.rem(g, X)
            z_at = jnp.where(lax.rem(x, 2) == 0, z, 12 + lax.rem(z + 4, 12))
            rows[t * G : (t + 1) * G, :] = b[p, lax.div(x, 2) * 24 + z_at]
        half = jnp.dot(rows[...], d[...], preferred_element_type=jnp.float32).astype(jnp.bfloat16)
        full = b[p].reshape(A, A)
        acc[...] += lax.dot_general(
            half, full, (((1,), (1,)), ((), ())), preferred_element_type=jnp.float32
        )
    lane = lax.broadcasted_iota(jnp.int32, (ROWS // 2, 128), 1)
    for y in range(Y):
        for q in range(X // 2):
            block = acc[y * ROWS : (y + 1) * ROWS, q * HALF : (q + 1) * HALF]
            first, middle, last = block[:, :128], block[:, 128:256], block[:, 256:]
            turned = pltpu.roll(middle, 64, 1)
            top, bottom = slice(0, ROWS // 2), slice(ROWS // 2, ROWS)
            even = jnp.where(lane < 64, middle[top], turned[bottom])
            odd = jnp.where(lane < 64, turned[top], middle[bottom])
            out_ref[(2 * q) * Y + y] = jnp.concatenate([first, even], 0).astype(jnp.bfloat16)
            out_ref[(2 * q + 1) * Y + y] = jnp.concatenate([last, odd], 0).astype(jnp.bfloat16)


def exchange_rows(core, d_pattern, d_own, d_other, b_own, b_other):
    count = b_own.shape[0]
    return pl.pallas_call(
        functools.partial(exchange_kernel, count),
        in_specs=[SMEM, SMEM, VMEM, VMEM, ANY, ANY],
        out_specs=VMEM,
        out_shape=jax.ShapeDtypeStruct((X * Y, PACK, 128), jnp.bfloat16),
        scratch_shapes=[
            pltpu.VMEM((2 * count, GROUPS, G, A), jnp.bfloat16),
            pltpu.VMEM((A, A), jnp.bfloat16),
            pltpu.VMEM((Y * ROWS, A), jnp.bfloat16),
            pltpu.VMEM((Y * ROWS, A), jnp.float32),
            pltpu.SemaphoreType.DMA((2 * count,)),
        ],
        compiler_params=pltpu.CompilerParams(vmem_limit_bytes=40 * 1024 * 1024),
        name="exchange",
    )(core, d_pattern, d_own, d_other, b_own, b_other)


def sum_xy_kernel(in_ref, out_ref):
    total = in_ref[0].astype(jnp.float32)
    for i in range(1, X * Y):
        total = total + in_ref[i].astype(jnp.float32)
    first, rest = total[:ROWS], total[ROWS:]
    first = first.T
    rest = rest.T
    rest = jnp.concatenate([rest[:64], rest[64:]], 1)
    for i in range(Z * C):
        part = first[i * K : (i + 1) * K] if i < MAIN * C else rest[i * K - 128 : (i + 1) * K - 128]
        out_ref[i] = part


def sum_xy(parts):
    return pl.pallas_call(
        sum_xy_kernel,
        in_specs=[VMEM],
        out_specs=VMEM,
        out_shape=jax.ShapeDtypeStruct((Z * C, K, ROWS), jnp.float32),
        name="sum_xy",
    )(parts)


def sum_z_kernel(factor, in_ref, out_ref):
    halves = []
    for c in range(C):
        total = in_ref[c]
        for z in range(1, Z):
            total = total + in_ref[z * C + c]
        halves.append(total * factor)
    out_ref[...] = jnp.concatenate(halves, 1)


def sum_z(parts, factor):
    return pl.pallas_call(
        functools.partial(sum_z_kernel, factor),
        in_specs=[VMEM],
        out_specs=VMEM,
        out_shape=jax.ShapeDtypeStruct((K, C * ROWS), jnp.float32),
        name="sum_z",
    )(parts)


def per_device(three_center, b_pattern, density, d_pattern):
    core = lax.axis_index("c")
    swap = [(0, 1), (1, 0)]
    b_own = mask_and_order(three_center, b_pattern)
    b_other = lax.ppermute(b_own, "c", swap)
    mine = lax.dynamic_slice(density, (0, core * HALF), (density.shape[0], HALF))
    mine = jnp.broadcast_to(mine[None], (Y,) + mine.shape)
    d_own = lax.all_to_all(mine, "y", 0, 0, tiled=True).reshape(A, HALF)
    d_other = lax.ppermute(d_own, "c", swap)
    parts = exchange_rows(core.reshape(1), d_pattern, d_own, d_other, b_own, b_other)
    parts = lax.all_to_all(parts, ("x", "y"), 0, 0, tiled=True)
    parts = lax.all_to_all(sum_xy(parts), ("z", "c"), 0, 0, tiled=True)
    total_ri = three_center.shape[0] * Z * X * C * Y
    return sum_z(parts, 1.0 / math.sqrt(total_ri * A)).T


def solution(mesh):
    fine = Mesh(mesh.devices.reshape(Z, X, C, Y), ("z", "x", "c", "y"))
    every = ("z", "x", "c", "y")
    return jax.shard_map(
        per_device,
        mesh=fine,
        in_specs=(P(every, None, None), P(every, None, None), P("y", None), P()),
        out_specs=P("y", ("z", "x", "c")),
        check_vma=False,
    )
```

time: 333 us -> 102 us (0.31)
  waiting for transfers between devices: 296 us -> 1.61 us
  blocking collectives: 0 us -> 65.2 us
  starting transfers between devices: 0.08 us -> 14.7 us
  Pallas kernels: 0 us -> 13.4 us
  between operations: 13.1 us -> 0.08 us
  matrix products: 11.2 us -> 0 us
    reduce_scatter x1 -> x0, waiting for transfers between devices: 206 us -> none  [per_device(): lax.psum_scatter(partial_value, 'ri', scatter_dimension=1, tiled=True)]
    all_to_all x0 -> x3, blocking collectives: none -> 65.2 us  [the longest x1 23.9 us: per_device(): parts = lax.all_to_all(sum_xy(parts), ('z', 'c'), 0, 0, tiled=True)]
    unnamed x4 -> x0, waiting for transfers between devices: 45.3 us -> none
    all_gather x1 -> x0, waiting for transfers between devices: 44.3 us -> none  [per_device(): rows_in = lax.all_gather(density, 'ao', axis=0, tiled=True)]
    ppermute x0 -> x2, starting transfers between devices: none -> 14.7 us  [the longest x1 12.4 us: per_device(): b_other = lax.ppermute(b_own, 'c', swap)]
    pallas_call x0 -> x4, Pallas kernels: none -> 13.4 us  [the longest x1 6.94 us: exchange_rows(): pl.pallas_call(functools.partial(exchange_kernel, count), in_specs=[SMEM,...]
    dot_general x2 -> x0, matrix products: 11.2 us -> none  [the longest x1 7.17 us: per_device(): jnp.einsum('pms,pns->mn', half, masked_b, preferred_element_type=jnp.floa...]
    broadcast_in_dim x2 -> x1, local copies, waits for them, and re-layouts: 3.55 us -> 0.05 us  [per_device(): mine = jnp.broadcast_to(mine[None], (Y,) + mine.shape)]
  transfers between devices with their start and end apart: 3 -> 2, of which waited for: 3 -> 1; matrix products, arithmetic and copies ran while one was open for 2% -> 0% of each run, Pallas kernels for 0% -> 0%
where the time goes in v1:
time: 102 us; the launch traced here: 101 us
  blocking collectives  65.2 us (64%)
  starting transfers between devices  14.7 us (14%)
  Pallas kernels  13.4 us (13%)
  local copies, waits for them, and re-layouts  5.31 us (5%)
  waiting for transfers between devices  1.61 us (2%)
    all_to_all x1, blocking collectives, per_device(): parts = lax.all_to_all(sum_xy(parts), ('z', 'c'), 0, 0, tiled=True)  23.9 us
    all_to_all x1, blocking collectives, per_device(): d_own = lax.all_to_all(mine, 'y', 0, 0, tiled=True).reshape(A, HALF)  21.8 us
    all_to_all x1, blocking collectives, per_device(): parts = lax.all_to_all(parts, ('x', 'y'), 0, 0, tiled=True)  19.5 us
    ppermute x1, starting transfers between devices, per_device(): b_other = lax.ppermute(b_own, 'c', swap)  12.4 us
    pallas_call x1, Pallas kernels, exchange_rows(): pl.pallas_call(functools.partial(exchange_kernel, count), in_specs=[SMEM,...  6.94 us
    unnamed x9, local copies, waits for them, and re-layouts  4.73 us
    pallas_call x1, Pallas kernels, mask_and_order(): pl.pallas_call(mask_kernel, grid=(count,), in_specs=[SMEM, spec], out_spe...  2.98 us
    ppermute x1, starting transfers between devices, per_device(): d_other = lax.ppermute(d_own, 'c', swap)  2.34 us
  transfers between devices with their start and end apart: 2, of which 1 were waited for; matrix products, arithmetic and copies ran while one was open for 0% of the time, Pallas kernels for 0%

profile of v1, /device:TPU:1, one launch (start us, length us, event | category | flops | bytes accessed | tf_op | source)
XLA Modules:
  0.0 101.0 jit_solution(17454266117752533760)
XLA Ops:
  0.0 0.0 copy-start
  0.0 1.3 %copy.5.pattern = s32[2,6,6]{2,1,0:T(8,128)} copy(s32[2,6,6]{2,0,1:T(2,128)} %param.5) | data formatting | bytes 576 | tf_op args[1]
  1.3 0.0 copy-start.2
  1.3 3.0 %mask.1.b_own = bf16[2,48,16,768]{3,2,1,0:T(8,128)(2,1)} custom-call(s32[2,6,6]{2,1,0:T(8,128)} %copy.5.pattern, bf16[2,48,16,768]{3,2,1,0:T(8,128)(2,1)} %bitcast.6), custom_call_target="tpu_custom_call" | custom-call | tf_op jit(solution)/shard_map/mask/pallas_call | solution.py:43
  4.3 12.4 %collective-permute-start.1 = (bf16[2,48,16,768]{3,2,1,0:T(8,128)(2,1)}, bf16[2,48,16,768]{3,2,1,0:T(8,128)(2,1)S(1)}, u32[]{:S(2)}, u32[]{:S(2)}) collective-permute-start(bf16[2,48,16,768]{3,2,1,0:T(8,128)(2,1)} %mask.1.b_own), channel_id=1, source_target_pairs={{0,8},{8,0},{1,9},{9,1},{2,10},{10,2},{3,11},{11,3},{4,12},{12,4},... | collective-permute-start | bytes 7077896 | tf_op jit(solution)/shard_map/ppermute | solution.py:163
  16.7 0.0 copy-done
  16.8 0.1 broadcast_in_dim.2
  16.8 21.8 %all_to_all.15 = bf16[8,96,384]{2,1,0:T(8,128)(2,1)S(1)} all-to-all(bf16[8,96,384]{2,1,0:T(8,128)(2,1)S(1)} %broadcast_in_dim.2), channel_id=1, replica_groups=mesh['z'=12,'x'=4,'c'=2,'y'=8] {'y'}, dimensions={0} | all-to-all | bytes 1179648 | tf_op jit(solution)/shard_map/all_to_all | solution.py:166
  38.6 2.3 %collective-permute-start = (bf16[768,384]{1,0:T(8,128)(2,1)S(1)}, bf16[768,384]{1,0:T(8,128)(2,1)S(1)}, u32[]{:S(2)}, u32[]{:S(2)}) collective-permute-start(bf16[768,384]{1,0:T(8,128)(2,1)S(1)} %bitcast.4), channel_id=1, source_target_pairs={{0,8},{8,0},{1,9},{9,1},{2,10},{10,2},{3,11},{11,3},{4,12},{12,4},... | collective-permute-start | bytes 1769480 | tf_op jit(solution)/shard_map/ppermute | solution.py:167
  41.0 1.6 %collective-permute-done.d_other = bf16[768,384]{1,0:T(8,128)(2,1)S(1)} collective-permute-done((bf16[768,384]{1,0:T(8,128)(2,1)S(1)}, bf16[768,384]{1,0:T(8,128)(2,1)S(1)}, u32[]{:S(2)}, u32[]{:S(2)}) %collective-permute-start) | collective-permute-done | bytes 589856 | tf_op jit(solution)/shard_map/ppermute | solution.py:167
  42.6 0.0 collective-permute-done.1.b_other
  42.6 0.0 copy-done.2
  42.6 0.0 copy-start.1
  42.6 1.7 %copy-done.1 = bf16[2,48,16,768]{3,2,1,0:T(8,128)(2,1)S(1)} copy-done((bf16[2,48,16,768]{3,2,1,0:T(8,128)(2,1)S(1)}, bf16[2,48,16,768]{3,2,1,0:T(8,128)(2,1)}, u32[]{:S(2)}) %copy-start.1) | copy-done | bytes 2359320
  44.2 6.9 %exchange.1 = bf16[32,72,128]{2,1,0:T(8,128)(2,1)S(1)} custom-call(s32[1]{0:T(128)} %bitcast.core_ref, s32[6,6]{1,0:T(8,128)S(1)} %copy-done.2, bf16[768,384]{1,0:T(8,128)(2,1)S(1)} %bitcast.5, bf16[768,384]{1,0:T(8,128)(2,1)S(1)} %collective-permute-done.d_other, bf16[2,48,16,768]{3,2,1,0:T(8,128)(2,1)S(1)} %copy-done.1, ...), custom_call_target="tpu_custom_call" | custom-call | tf_op jit(solution)/shard_map/exchange/pallas_call | solution.py:99
  51.2 19.5 %all_to_all.16.in_ref = bf16[32,72,128]{2,1,0:T(8,128)(2,1)} all-to-all(bf16[32,72,128]{2,1,0:T(8,128)(2,1)S(1)} %exchange.1), channel_id=1, replica_groups=mesh['z'=12,'x'=4,'c'=2,'y'=8] {'x','y'}, dimensions={0} | all-to-all | bytes 1179648 | tf_op jit(solution)/shard_map/all_to_all | solution.py:169
  70.6 1.9 %sum_xy.1 = f32[24,8,48]{2,1,0:T(8,128)} custom-call(bf16[32,72,128]{2,1,0:T(8,128)(2,1)} %all_to_all.16.in_ref), custom_call_target="tpu_custom_call" | custom-call | tf_op jit(solution)/shard_map/sum_xy/pallas_call | solution.py:130
  72.5 1.0 %reshape.13 = f32[24,1,384]{2,1,0:T(1,128)S(1)} reshape(f32[24,8,48]{2,1,0:T(8,128)} %sum_xy.1) | data formatting | bytes 73728
  73.6 23.9 %all_to_all.17 = f32[24,1,384]{2,1,0:T(1,128)S(1)} all-to-all(f32[24,1,384]{2,1,0:T(1,128)S(1)} %reshape.13), channel_id=1, replica_groups=mesh['z'=12,'x'=4,'c'=2,'y'=8] {'z','c'}, dimensions={0} | all-to-all | bytes 73728 | tf_op jit(solution)/shard_map/all_to_all | solution.py:170
  97.5 0.5 broadcast.1
  98.0 0.7 reduce
  98.7 0.7 reshape.14.in_ref
  99.5 1.6 %sum_z.1 = f32[8,96]{1,0:T(8,128)} custom-call(f32[24,8,48]{2,1,0:T(8,128)} %reshape.14.in_ref), custom_call_target="tpu_custom_call" | custom-call | tf_op jit(solution)/shard_map/sum_z/pallas_call | solution.py:150
  (1 shorter events, 0.0 us)
Async XLA Ops:
  0.0 16.7 %copy-start = (bf16[96,768]{1,0:T(8,128)(2,1)S(1)}, bf16[96,768]{1,0:T(8,128)(2,1)}, u32[]{:S(2)}) copy-start(bf16[96,768]{1,0:T(8,128)(2,1)} %param.6) | copy-start | bytes 442372
  1.3 41.3 %copy-start.2 = (s32[6,6]{1,0:T(8,128)S(1)}, s32[6,6]{1,0:T(8,128)}, u32[]{:S(2)}) copy-start(s32[6,6]{1,0:T(8,128)} %d_pattern.1) | copy-start | bytes 436
  4.3 38.3 %collective-permute-start.1 = (bf16[2,48,16,768]{3,2,1,0:T(8,128)(2,1)}, bf16[2,48,16,768]{3,2,1,0:T(8,128)(2,1)S(1)}, u32[]{:S(2)}, u32[]{:S(2)}) collective-permute-start(bf16[2,48,16,768]{3,2,1,0:T(8,128)(2,1)} %mask.1.b_own), channel_id=1, source_target_pairs={{0,8},{8,0},{1,9},{9,1},{2,10},{10,2},{3,11},{11,3},{4,12},{12,4},... | collective-permute-start | bytes 7077896 | tf_op jit(solution)/shard_map/ppermute | solution.py:163
  38.6 4.0 %collective-permute-start = (bf16[768,384]{1,0:T(8,128)(2,1)S(1)}, bf16[768,384]{1,0:T(8,128)(2,1)S(1)}, u32[]{:S(2)}, u32[]{:S(2)}) collective-permute-start(bf16[768,384]{1,0:T(8,128)(2,1)S(1)} %bitcast.4), channel_id=1, source_target_pairs={{0,8},{8,0},{1,9},{9,1},{2,10},{10,2},{3,11},{11,3},{4,12},{12,4},... | collective-permute-start | bytes 1769480 | tf_op jit(solution)/shard_map/ppermute | solution.py:167
  42.6 1.7 %copy-start.1 = (bf16[2,48,16,768]{3,2,1,0:T(8,128)(2,1)S(1)}, bf16[2,48,16,768]{3,2,1,0:T(8,128)(2,1)}, u32[]{:S(2)}) copy-start(bf16[2,48,16,768]{3,2,1,0:T(8,128)(2,1)} %mask.1.b_own) | copy-start | bytes 7077892

commit v2 on v1

v2 whole, which is shorter than its diff:
```python
import functools
import math

import jax
import jax.numpy as jnp
from jax import lax
from jax.experimental import pallas as pl
from jax.experimental.pallas import tpu as pltpu
from jax.sharding import Mesh, PartitionSpec as P

Z, X, C, Y = 12, 4, 2, 8
A, BS, NB = 768, 128, 6
K = 8
G = 16
GROUPS = A // G
ROWS = A // (Y * C)
YROWS = A // Y
STEP = 32
SENT = 4
PACK = ROWS * Z * G // 128
MAIN = 128 // G
VMEM = pl.BlockSpec(memory_space=pltpu.VMEM)
SMEM = pl.BlockSpec(memory_space=pltpu.SMEM)
ANY = pl.BlockSpec(memory_space=pl.ANY)


def place(z, x):
    return (x // 2) * 24 + (z if x % 2 == 0 else 12 + (z + 4) % 12)


def mask_kernel(pattern, b_ref, out_ref):
    p = pl.program_id(0)
    for rb in range(NB):
        for cb in range(NB):
            keep = pattern[rb, p, cb] > 0
            lanes = slice(cb * BS, (cb + 1) * BS)
            for g in range(rb * 8, rb * 8 + 8):
                block = b_ref[0, g, :, lanes]
                out_ref[0, place(g // X, g % X), :, lanes] = jnp.where(keep, block, jnp.zeros_like(block))


def mask_and_order(three_center, b_pattern):
    count = three_center.shape[0]
    spec = pl.BlockSpec((1, GROUPS, G, A), lambda p: (p, 0, 0, 0))
    return pl.pallas_call(
        mask_kernel,
        grid=(count,),
        in_specs=[SMEM, spec],
        out_specs=spec,
        out_shape=pltpu.VMEM((count, GROUPS, G, A), jnp.bfloat16),
        name="mask",
    )(b_pattern.transpose(1, 0, 2), three_center.reshape(count, GROUPS, G, A))


def exchange_kernel(count, core_ref, d_pattern, d_own, d_other, b_own, b_other, out_ref, d, acc):
    core = core_ref[0]
    for h, part in ((core, d_own), (1 - core, d_other)):
        for y in range(Y):
            for t in range(YROWS // STEP):
                rb = (y * YROWS + t * STEP) // BS
                here = slice(y * YROWS + t * STEP, y * YROWS + (t + 1) * STEP)
                for j in range(SENT // C):
                    col = lax.rem(rb + h * (SENT // C) + j, NB)
                    keep = jnp.maximum(d_pattern[rb, col], d_pattern[col, rb]) > 0
                    block = part[y, t * STEP : (t + 1) * STEP, j * BS : (j + 1) * BS]
                    lanes = pl.ds(pl.multiple_of(col * BS, BS), BS)
                    d[here, lanes] = jnp.where(keep, block, jnp.zeros_like(block))
    for rb in range(NB):
        for k in range(SENT, NB):
            cb = (rb + k) % NB
            rows, cols = slice(rb * BS, (rb + 1) * BS), slice(cb * BS, (cb + 1) * BS)
            d[rows, cols] = d[cols, rows].T
    for p in range(2 * count):
        b = b_own.at[p] if p < count else b_other.at[p - count]
        full = b[...].reshape(A, A)
        for q in range(X // 2):
            rows = b[pl.ds(q * 2 * Z + core * Z, Z)].reshape(Z * G, A)
            half = jnp.dot(rows, d[...], preferred_element_type=jnp.float32).astype(jnp.bfloat16)
            term = lax.dot_general(half, full, (((1,), (1,)), ((), ())), preferred_element_type=jnp.float32)
            here = slice(q * Z * G, (q + 1) * Z * G)
            acc[here, :] = term if p == 0 else acc[here, :] + term
    lane = lax.broadcasted_iota(jnp.int32, (ROWS // 2, 128), 1)
    top, bottom = slice(0, ROWS // 2), slice(ROWS // 2, ROWS)
    for y in range(Y):
        groups = []
        for t in range(ROWS // G):
            g = y * (YROWS // G) + 2 * t
            z, q = g // X, (g % X) // 2
            at = q * Z + jnp.where(core == 0, z, (z + Z - MAIN) % Z)
            groups.append(acc[pl.ds(pl.multiple_of(at * G, G), G), :])
        for q in range(X // 2):
            first, middle, last = [
                jnp.concatenate([g[:, (3 * q + i) * 128 : (3 * q + i + 1) * 128] for g in groups], 0)
                for i in range(3)
            ]
            turned = pltpu.roll(middle, 64, 1)
            even = jnp.where(lane < 64, middle[top], turned[bottom])
            odd = jnp.where(lane < 64, turned[top], middle[bottom])
            out_ref[(2 * q) * Y + y] = jnp.concatenate([first, even], 0).astype(jnp.bfloat16)
            out_ref[(2 * q + 1) * Y + y] = jnp.concatenate([last, odd], 0).astype(jnp.bfloat16)


def exchange_rows(core, d_pattern, d_own, d_other, b_own, b_other):
    count = b_own.shape[0]
    return pl.pallas_call(
        functools.partial(exchange_kernel, count),
        in_specs=[SMEM, SMEM, VMEM, VMEM, VMEM, VMEM],
        out_specs=VMEM,
        out_shape=pltpu.VMEM((X * Y, PACK, 128), jnp.bfloat16),
        scratch_shapes=[
            pltpu.VMEM((A, A), jnp.bfloat16),
            pltpu.VMEM((Y * ROWS, A), jnp.float32),
        ],
        compiler_params=pltpu.CompilerParams(vmem_limit_bytes=40 * 1024 * 1024),
        name="exchange",
    )(core, d_pattern, d_own, d_other, b_own, pltpu.with_memory_space_constraint(b_other, pltpu.VMEM))


def pack_kernel(place_ref, density, out_ref):
    y, core = place_ref[0], place_ref[1]
    for t in range(YROWS // STEP):
        rb = lax.div(y * YROWS + t * STEP, BS)
        for j in range(SENT // C):
            col = lax.rem(rb + core * (SENT // C) + j, NB)
            block = density[t * STEP : (t + 1) * STEP, pl.ds(pl.multiple_of(col * BS, BS), BS)]
            for to in range(Y):
                out_ref[to, t * STEP : (t + 1) * STEP, j * BS : (j + 1) * BS] = block


def pack_density(place_at, density):
    return pl.pallas_call(
        pack_kernel,
        in_specs=[SMEM, VMEM],
        out_specs=VMEM,
        out_shape=pltpu.VMEM((Y, YROWS, SENT // C * BS), jnp.bfloat16),
        name="pack",
    )(place_at, density)


def sum_xy_kernel(in_ref, out_ref):
    total = in_ref[0].astype(jnp.float32)
    for i in range(1, X * Y):
        total = total + in_ref[i].astype(jnp.float32)
    first, rest = total[:ROWS], total[ROWS:]
    first = first.T
    rest = rest.T
    rest = jnp.concatenate([rest[:64], rest[64:]], 1)
    both = jnp.concatenate([first, rest], 0)
    both = jnp.concatenate([both, jnp.zeros((Z * G, 128 - ROWS), jnp.float32)], 1)
    out_ref[...] = both.reshape(Z * C, K, 128)


def sum_xy(parts):
    return pl.pallas_call(
        sum_xy_kernel,
        in_specs=[VMEM],
        out_specs=VMEM,
        out_shape=pltpu.VMEM((Z * C, K, 128), jnp.float32),
        name="sum_xy",
    )(pltpu.with_memory_space_constraint(parts, pltpu.VMEM))


def sum_z_kernel(factor, in_ref, out_ref):
    halves = []
    for c in range(C):
        total = in_ref[c]
        for z in range(1, Z):
            total = total + in_ref[z * C + c]
        halves.append(total * factor)
    out_ref[...] = jnp.concatenate([halves[g % C][:, g // C * G : (g // C + 1) * G] for g in range(YROWS // G)], 1)


def sum_z(parts, factor):
    return pl.pallas_call(
        functools.partial(sum_z_kernel, factor),
        in_specs=[VMEM],
        out_specs=VMEM,
        out_shape=jax.ShapeDtypeStruct((K, YROWS), jnp.float32),
        name="sum_z",
    )(pltpu.with_memory_space_constraint(parts, pltpu.VMEM))


def per_device(three_center, b_pattern, density, d_pattern):
    core, y = lax.axis_index("c"), lax.axis_index("y")
    swap = [(0, 1), (1, 0)]
    mine = pack_density(jnp.stack([y, core]), density)
    mine, b_pattern = lax.optimization_barrier((mine, b_pattern))
    b_own = mask_and_order(three_center, b_pattern)
    b_other = lax.ppermute(b_own, "c", swap)
    d_own = lax.all_to_all(mine, "y", 0, 0, tiled=True)
    d_other = lax.ppermute(d_own, "c", swap)
    parts = exchange_rows(core.reshape(1), d_pattern, d_own, d_other, b_own, b_other)
    parts = lax.all_to_all(parts, ("x", "y"), 0, 0, tiled=True)
    parts = lax.all_to_all(sum_xy(parts), ("z", "c"), 0, 0, tiled=True)
    total_ri = three_center.shape[0] * Z * X * C * Y
    return sum_z(parts, 1.0 / math.sqrt(total_ri * A)).T


def solution(mesh):
    fine = Mesh(mesh.devices.reshape(Z, X, C, Y), ("z", "x", "c", "y"))
    every = ("z", "x", "c", "y")
    return jax.shard_map(
        per_device,
        mesh=fine,
        in_specs=(P(every, None, None), P(every, None, None), P("y", None), P()),
        out_specs=P("y", ("z", "x", "c")),
        check_vma=False,
    )
```

time: 102 us -> 89.4 us (0.88)
  local copies, waits for them, and re-layouts: 5.31 us -> 0.01 us
  Pallas kernels: 13.4 us -> 9.93 us
  blocking collectives: 65.2 us -> 62 us
    unnamed x9 -> x2, local copies, waits for them, and re-layouts: 4.73 us -> 0.01 us
    all_to_all x1, blocking collectives: 21.8 us -> 17.6 us  [per_device(): d_own = lax.all_to_all(mine, 'y', 0, 0, tiled=True)]
    all_to_all x1, blocking collectives: 23.9 us -> 25.6 us  [per_device(): parts = lax.all_to_all(sum_xy(parts), ('z', 'c'), 0, 0, tiled=True)]
    pallas_call x1, Pallas kernels: 1.9 us -> 0.21 us  [sum_xy(): pl.pallas_call(sum_xy_kernel, in_specs=[VMEM], out_specs=VMEM, out_shape=...]
    pallas_call x1, Pallas kernels: 2.98 us -> 1.94 us  [mask_and_order(): pl.pallas_call(mask_kernel, grid=(count,), in_specs=[SMEM, spec], out_spe...]
where the time goes in v2:
time: 89.4 us; the launch traced here: 88.7 us
  blocking collectives  62 us (69%)
  starting transfers between devices  14.8 us (17%)
  Pallas kernels  9.93 us (11%)
  waiting for transfers between devices  1.33 us (1%)
    all_to_all x1, blocking collectives, per_device(): parts = lax.all_to_all(sum_xy(parts), ('z', 'c'), 0, 0, tiled=True)  25.6 us
    all_to_all x1, blocking collectives, per_device(): parts = lax.all_to_all(parts, ('x', 'y'), 0, 0, tiled=True)  18.8 us
    all_to_all x1, blocking collectives, per_device(): d_own = lax.all_to_all(mine, 'y', 0, 0, tiled=True)  17.6 us
    ppermute x1, starting transfers between devices, per_device(): b_other = lax.ppermute(b_own, 'c', swap)  12.4 us
    pallas_call x1, Pallas kernels, exchange_rows(): pl.pallas_call(functools.partial(exchange_kernel, count), in_specs=[SMEM,...  6.12 us
    ppermute x1, starting transfers between devices, per_device(): d_other = lax.ppermute(d_own, 'c', swap)  2.34 us
    pallas_call x1, Pallas kernels, mask_and_order(): pl.pallas_call(mask_kernel, grid=(count,), in_specs=[SMEM, spec], out_spe...  1.94 us
  transfers between devices with their start and end apart: 2, of which 1 were waited for; matrix products, arithmetic and copies ran while one was open for 0% of the time, Pallas kernels for 0%

profile of v2, /device:TPU:1, one launch (start us, length us, event | category | flops | bytes accessed | tf_op | source)
XLA Modules:
  0.0 88.7 jit_solution(7122614735107867242)
XLA Ops:
  0.0 0.6 pad_add_fusion.place_ref
  0.6 1.0 %pack.1 = bf16[8,96,256]{2,1,0:T(8,128)(2,1)S(1)} custom-call(s32[2]{0:T(128)} %pad_add_fusion.place_ref, bf16[96,768]{1,0:T(8,128)(2,1)} %density.1), custom_call_target="tpu_custom_call" | custom-call | tf_op jit(solution)/shard_map/pack/pallas_call | solution.py:131
  1.6 0.0 copy-start
  1.6 1.9 %mask.1.b_own = bf16[2,48,16,768]{3,2,1,0:T(8,128)(2,1)S(1)} custom-call(s32[6,2,6]{2,1,0:T(2,128)} %bitcast.6, bf16[2,48,16,768]{3,2,1,0:T(8,128)(2,1)} %bitcast.5), custom_call_target="tpu_custom_call" | custom-call | tf_op jit(solution)/shard_map/mask/pallas_call | solution.py:45
  3.6 12.4 %collective-permute-start.1 = (bf16[2,48,16,768]{3,2,1,0:T(8,128)(2,1)S(1)}, bf16[2,48,16,768]{3,2,1,0:T(8,128)(2,1)S(1)}, u32[]{:S(2)}, u32[]{:S(2)}) collective-permute-start(bf16[2,48,16,768]{3,2,1,0:T(8,128)(2,1)S(1)} %mask.1.b_own), channel_id=1, source_target_pairs={{0,8},{8,0},{1,9},{9,1},{2,10},{10,2},{3,11},{11,3},{4,12},{12,4},... | collective-permute-start | bytes 7077896 | tf_op jit(solution)/shard_map/ppermute | solution.py:189
  16.0 17.6 %all_to_all.15.d_own = bf16[8,96,256]{2,1,0:T(8,128)(2,1)S(1)} all-to-all(bf16[8,96,256]{2,1,0:T(8,128)(2,1)S(1)} %pack.1), channel_id=1, replica_groups=mesh['z'=12,'x'=4,'c'=2,'y'=8] {'y'}, dimensions={0} | all-to-all | bytes 786432 | tf_op jit(solution)/shard_map/all_to_all | solution.py:190
  33.6 2.3 %collective-permute-start = (bf16[8,96,256]{2,1,0:T(8,128)(2,1)S(1)}, bf16[8,96,256]{2,1,0:T(8,128)(2,1)S(1)}, u32[]{:S(2)}, u32[]{:S(2)}) collective-permute-start(bf16[8,96,256]{2,1,0:T(8,128)(2,1)S(1)} %all_to_all.15.d_own), channel_id=1, source_target_pairs={{0,8},{8,0},{1,9},{9,1},{2,10},{10,2},{3,11},{11,3},{4,12},{12,4},... | collective-permute-start | bytes 1179656 | tf_op jit(solution)/shard_map/ppermute | solution.py:191
  35.9 1.3 %collective-permute-done.d_other = bf16[8,96,256]{2,1,0:T(8,128)(2,1)S(1)} collective-permute-done((bf16[8,96,256]{2,1,0:T(8,128)(2,1)S(1)}, bf16[8,96,256]{2,1,0:T(8,128)(2,1)S(1)}, u32[]{:S(2)}, u32[]{:S(2)}) %collective-permute-start) | collective-permute-done | bytes 393248 | tf_op jit(solution)/shard_map/ppermute | solution.py:191
  37.3 0.0 collective-permute-done.1.b_other
  37.3 0.0 copy-done
  37.3 6.1 %exchange.1 = bf16[32,72,128]{2,1,0:T(8,128)(2,1)S(1)} custom-call(s32[1]{0:T(128)} %bitcast.core_ref, s32[6,6]{1,0:T(8,128)S(1)} %copy-done, bf16[8,96,256]{2,1,0:T(8,128)(2,1)S(1)} %all_to_all.15.d_own, bf16[8,96,256]{2,1,0:T(8,128)(2,1)S(1)} %collective-permute-done.d_other, bf16[2,48,16,768]{3,2,1,0:T(8,128)(2,1)S(1)} %mask.1.b_own, ...), custom_call_target="tpu_custom_call" | custom-call | tf_op jit(solution)/shard_map/exchange/pallas_call | solution.py:105
  43.4 18.8 %all_to_all.16.in_ref = bf16[32,72,128]{2,1,0:T(8,128)(2,1)S(1)} all-to-all(bf16[32,72,128]{2,1,0:T(8,128)(2,1)S(1)} %exchange.1), channel_id=1, replica_groups=mesh['z'=12,'x'=4,'c'=2,'y'=8] {'x','y'}, dimensions={0} | all-to-all | bytes 1179648 | tf_op jit(solution)/shard_map/all_to_all | solution.py:193
  62.2 0.2 sum_xy.1
  62.4 25.6 %all_to_all.17.in_ref = f32[24,8,128]{2,1,0:T(8,128)S(1)} all-to-all(f32[24,8,128]{2,1,0:T(8,128)S(1)} %sum_xy.1), channel_id=1, replica_groups=mesh['z'=12,'x'=4,'c'=2,'y'=8] {'z','c'}, dimensions={0} | all-to-all | bytes 196608 | tf_op jit(solution)/shard_map/all_to_all | solution.py:194
  88.0 0.7 sum_z.1
Async XLA Ops:
  1.6 35.7 %copy-start = (s32[6,6]{1,0:T(8,128)S(1)}, s32[6,6]{1,0:T(8,128)}, u32[]{:S(2)}) copy-start(s32[6,6]{1,0:T(8,128)} %d_pattern.1) | copy-start | bytes 436
  3.6 33.7 %collective-permute-start.1 = (bf16[2,48,16,768]{3,2,1,0:T(8,128)(2,1)S(1)}, bf16[2,48,16,768]{3,2,1,0:T(8,128)(2,1)S(1)}, u32[]{:S(2)}, u32[]{:S(2)}) collective-permute-start(bf16[2,48,16,768]{3,2,1,0:T(8,128)(2,1)S(1)} %mask.1.b_own), channel_id=1, source_target_pairs={{0,8},{8,0},{1,9},{9,1},{2,10},{10,2},{3,11},{11,3},{4,12},{12,4},... | collective-permute-start | bytes 7077896 | tf_op jit(solution)/shard_map/ppermute | solution.py:189
  33.6 3.7 %collective-permute-start = (bf16[8,96,256]{2,1,0:T(8,128)(2,1)S(1)}, bf16[8,96,256]{2,1,0:T(8,128)(2,1)S(1)}, u32[]{:S(2)}, u32[]{:S(2)}) collective-permute-start(bf16[8,96,256]{2,1,0:T(8,128)(2,1)S(1)} %all_to_all.15.d_own), channel_id=1, source_target_pairs={{0,8},{8,0},{1,9},{9,1},{2,10},{10,2},{3,11},{11,3},{4,12},{12,4},... | collective-permute-start | bytes 1179656 | tf_op jit(solution)/shard_map/ppermute | solution.py:191

commit v3 on v2

--- a/solution.py
+++ b/solution.py
@@ -19,6 +19,8 @@
 SENT = 4
 PACK = ROWS * Z * G // 128
 MAIN = 128 // G
+COST = 10**11
+MIB = 1024 * 1024
 VMEM = pl.BlockSpec(memory_space=pltpu.VMEM)
 SMEM = pl.BlockSpec(memory_space=pltpu.SMEM)
 ANY = pl.BlockSpec(memory_space=pl.ANY)
@@ -28,31 +30,32 @@
     return (x // 2) * 24 + (z if x % 2 == 0 else 12 + (z + 4) % 12)
 
 
-def mask_kernel(pattern, b_ref, out_ref):
-    p = pl.program_id(0)
-    for rb in range(NB):
-        for cb in range(NB):
-            keep = pattern[rb, p, cb] > 0
-            lanes = slice(cb * BS, (cb + 1) * BS)
-            for g in range(rb * 8, rb * 8 + 8):
-                block = b_ref[0, g, :, lanes]
-                out_ref[0, place(g // X, g % X), :, lanes] = jnp.where(keep, block, jnp.zeros_like(block))
+def mask_kernel(count, pattern, b_ref, *out_refs):
+    for p in range(count):
+        for rb in range(NB):
+            for cb in range(NB):
+                keep = pattern[rb, p, cb] > 0
+                lanes = slice(cb * BS, (cb + 1) * BS)
+                for g in range(rb * 8, rb * 8 + 8):
+                    block = b_ref[p, g, :, lanes]
+                    q, at = divmod(place(g // X, g % X), 2 * Z)
+                    out_refs[p * (X // 2) + q][at, :, lanes] = jnp.where(keep, block, jnp.zeros_like(block))
 
 
 def mask_and_order(three_center, b_pattern):
     count = three_center.shape[0]
-    spec = pl.BlockSpec((1, GROUPS, G, A), lambda p: (p, 0, 0, 0))
-    return pl.pallas_call(
-        mask_kernel,
-        grid=(count,),
-        in_specs=[SMEM, spec],
-        out_specs=spec,
-        out_shape=pltpu.VMEM((count, GROUPS, G, A), jnp.bfloat16),
+    pieces = count * (X // 2)
+    return pl.pallas_call(
+        functools.partial(mask_kernel, count),
+        in_specs=[SMEM, VMEM],
+        out_specs=[VMEM] * pieces,
+        out_shape=[pltpu.VMEM((2 * Z, G, A), jnp.bfloat16)] * pieces,
+        compiler_params=pltpu.CompilerParams(vmem_limit_bytes=16 * MIB),
         name="mask",
     )(b_pattern.transpose(1, 0, 2), three_center.reshape(count, GROUPS, G, A))
 
 
-def exchange_kernel(count, core_ref, d_pattern, d_own, d_other, b_own, b_other, out_ref, d, acc):
+def density_kernel(core_ref, d_pattern, d_own, d_other, d):
     core = core_ref[0]
     for h, part in ((core, d_own), (1 - core, d_other)):
         for y in range(Y):
@@ -70,15 +73,34 @@
             cb = (rb + k) % NB
             rows, cols = slice(rb * BS, (rb + 1) * BS), slice(cb * BS, (cb + 1) * BS)
             d[rows, cols] = d[cols, rows].T
-    for p in range(2 * count):
-        b = b_own.at[p] if p < count else b_other.at[p - count]
-        full = b[...].reshape(A, A)
-        for q in range(X // 2):
-            rows = b[pl.ds(q * 2 * Z + core * Z, Z)].reshape(Z * G, A)
+
+
+def whole_density(core, d_pattern, d_own, d_other):
+    return pl.pallas_call(
+        density_kernel,
+        in_specs=[SMEM, SMEM, VMEM, VMEM],
+        out_specs=VMEM,
+        out_shape=pltpu.VMEM((A, A), jnp.bfloat16),
+        cost_estimate=pl.CostEstimate(flops=COST, bytes_accessed=0, transcendentals=0),
+        compiler_params=pltpu.CompilerParams(vmem_limit_bytes=8 * MIB),
+        name="density",
+    )(core, d_pattern, d_own, d_other)
+
+
+def exchange_kernel(core_ref, d, *refs):
+    *pieces, out_ref, acc = refs
+    core = core_ref[0]
+    halves = X // 2
+    for p in range(len(pieces) // halves):
+        for q in range(halves):
+            rows = pieces[p * halves + q][pl.ds(core * Z, Z)].reshape(Z * G, A)
             half = jnp.dot(rows, d[...], preferred_element_type=jnp.float32).astype(jnp.bfloat16)
-            term = lax.dot_general(half, full, (((1,), (1,)), ((), ())), preferred_element_type=jnp.float32)
             here = slice(q * Z * G, (q + 1) * Z * G)
-            acc[here, :] = term if p == 0 else acc[here, :] + term
+            for to in range(halves):
+                full = pieces[p * halves + to][...].reshape(2 * Z * G, A)
+                term = lax.dot_general(half, full, (((1,), (1,)), ((), ())), preferred_element_type=jnp.float32)
+                cols = slice(to * 2 * Z * G, (to + 1) * 2 * Z * G)
+                acc[here, cols] = term if p == 0 else acc[here, cols] + term
     lane = lax.broadcasted_iota(jnp.int32, (ROWS // 2, 128), 1)
     top, bottom = slice(0, ROWS // 2), slice(ROWS // 2, ROWS)
     for y in range(Y):
@@ -100,24 +122,21 @@
             out_ref[(2 * q + 1) * Y + y] = jnp.concatenate([last, odd], 0).astype(jnp.bfloat16)
 
 
-def exchange_rows(core, d_pattern, d_own, d_other, b_own, b_other):
-    count = b_own.shape[0]
-    return pl.pallas_call(
-        functools.partial(exchange_kernel, count),
-        in_specs=[SMEM, SMEM, VMEM, VMEM, VMEM, VMEM],
+def exchange_rows(core, d, pieces):
+    pieces = [pltpu.with_memory_space_constraint(piece, pltpu.VMEM) for piece in pieces]
+    return pl.pallas_call(
+        exchange_kernel,
+        in_specs=[SMEM, VMEM] + [VMEM] * len(pieces),
         out_specs=VMEM,
         out_shape=pltpu.VMEM((X * Y, PACK, 128), jnp.bfloat16),
-        scratch_shapes=[
-            pltpu.VMEM((A, A), jnp.bfloat16),
-            pltpu.VMEM((Y * ROWS, A), jnp.float32),
-        ],
-        compiler_params=pltpu.CompilerParams(vmem_limit_bytes=40 * 1024 * 1024),
+        scratch_shapes=[pltpu.VMEM((Y * ROWS, A), jnp.float32)],
+        compiler_params=pltpu.CompilerParams(vmem_limit_bytes=24 * MIB),
         name="exchange",
-    )(core, d_pattern, d_own, d_other, b_own, pltpu.with_memory_space_constraint(b_other, pltpu.VMEM))
-
-
-def pack_kernel(place_ref, density, out_ref):
-    y, core = place_ref[0], place_ref[1]
+    )(core, d, *pieces)
+
+
+def pack_kernel(y_ref, core_ref, density, out_ref):
+    y, core = y_ref[0], core_ref[0]
     for t in range(YROWS // STEP):
         rb = lax.div(y * YROWS + t * STEP, BS)
         for j in range(SENT // C):
@@ -127,14 +146,15 @@
                 out_ref[to, t * STEP : (t + 1) * STEP, j * BS : (j + 1) * BS] = block
 
 
-def pack_density(place_at, density):
+def pack_density(y, core, density):
     return pl.pallas_call(
         pack_kernel,
-        in_specs=[SMEM, VMEM],
+        in_specs=[SMEM, SMEM, VMEM],
         out_specs=VMEM,
         out_shape=pltpu.VMEM((Y, YROWS, SENT // C * BS), jnp.bfloat16),
+        compiler_params=pltpu.CompilerParams(vmem_limit_bytes=8 * MIB),
         name="pack",
-    )(place_at, density)
+    )(y, core, density)
 
 
 def sum_xy_kernel(in_ref, out_ref):
@@ -146,8 +166,9 @@
     rest = rest.T
     rest = jnp.concatenate([rest[:64], rest[64:]], 1)
     both = jnp.concatenate([first, rest], 0)
-    both = jnp.concatenate([both, jnp.zeros((Z * G, 128 - ROWS), jnp.float32)], 1)
-    out_ref[...] = both.reshape(Z * C, K, 128)
+    both = both.reshape(Z * C, K, ROWS)
+    pad = jnp.zeros((Z * C, K // 2, 128 - 2 * ROWS), jnp.float32)
+    out_ref[...] = jnp.concatenate([both[:, : K // 2], both[:, K // 2 :], pad], 2)
 
 
 def sum_xy(parts):
@@ -155,7 +176,8 @@
         sum_xy_kernel,
         in_specs=[VMEM],
         out_specs=VMEM,
-        out_shape=pltpu.VMEM((Z * C, K, 128), jnp.float32),
+        out_shape=pltpu.VMEM((Z * C, K // 2, 128), jnp.float32),
+        compiler_params=pltpu.CompilerParams(vmem_limit_bytes=8 * MIB),
         name="sum_xy",
     )(pltpu.with_memory_space_constraint(parts, pltpu.VMEM))
 
@@ -166,6 +188,7 @@
         total = in_ref[c]
         for z in range(1, Z):
             total = total + in_ref[z * C + c]
+        total = jnp.concatenate([total[:, :ROWS], total[:, ROWS : 2 * ROWS]], 0)
         halves.append(total * factor)
     out_ref[...] = jnp.concatenate([halves[g % C][:, g // C * G : (g // C + 1) * G] for g in range(YROWS // G)], 1)
 
@@ -176,20 +199,23 @@
         in_specs=[VMEM],
         out_specs=VMEM,
         out_shape=jax.ShapeDtypeStruct((K, YROWS), jnp.float32),
+        compiler_params=pltpu.CompilerParams(vmem_limit_bytes=4 * MIB),
         name="sum_z",
     )(pltpu.with_memory_space_constraint(parts, pltpu.VMEM))
 
 
 def per_device(three_center, b_pattern, density, d_pattern):
-    core, y = lax.axis_index("c"), lax.axis_index("y")
+    core, y = lax.axis_index("c").reshape(1), lax.axis_index("y").reshape(1)
     swap = [(0, 1), (1, 0)]
-    mine = pack_density(jnp.stack([y, core]), density)
+    mine = pack_density(y, core, density)
     mine, b_pattern = lax.optimization_barrier((mine, b_pattern))
     b_own = mask_and_order(three_center, b_pattern)
-    b_other = lax.ppermute(b_own, "c", swap)
+    b_other = [lax.ppermute(piece, "c", swap) for piece in b_own]
     d_own = lax.all_to_all(mine, "y", 0, 0, tiled=True)
+    d_own, *b_other = lax.optimization_barrier((d_own, *b_other))
     d_other = lax.ppermute(d_own, "c", swap)
-    parts = exchange_rows(core.reshape(1), d_pattern, d_own, d_other, b_own, b_other)
+    d = whole_density(core, d_pattern, d_own, d_other)
+    parts = exchange_rows(core, d, [*b_own, *b_other])
     parts = lax.all_to_all(parts, ("x", "y"), 0, 0, tiled=True)
     parts = lax.all_to_all(sum_xy(parts), ("z", "c"), 0, 0, tiled=True)
     total_ri = three_center.shape[0] * Z * X * C * Y

time: 89.4 us -> 91.4 us (1.022)
  blocking collectives: 62 us -> 47.7 us
  starting transfers between devices: 14.8 us -> 24.9 us
  local copies, waits for them, and re-layouts: 0.01 us -> 4.91 us
  waiting for transfers between devices: 1.33 us -> 2.9 us
    all_to_all x1 -> x0, blocking collectives: 17.6 us -> none  [per_device(): d_own = lax.all_to_all(mine, 'y', 0, 0, tiled=True)]
    all_to_all x0 -> x1, starting transfers between devices: none -> 7.65 us  [per_device(): d_own = lax.all_to_all(mine, 'y', 0, 0, tiled=True)]
    unnamed x2 -> x16, local copies, waits for them, and re-layouts: 0.01 us -> 4.91 us
    all_to_all x1, blocking collectives: 18.8 us -> 22.8 us  [per_device(): parts = lax.all_to_all(parts, ('x', 'y'), 0, 0, tiled=True)]
    ppermute x1 -> x4, starting transfers between devices: 12.4 us -> 15.1 us  [per_device(): b_other = [lax.ppermute(piece, 'c', swap) for piece in b_own]]
    ppermute x1 -> x4, waiting for transfers between devices: 0.01 us -> 1.13 us  [per_device(): b_other = [lax.ppermute(piece, 'c', swap) for piece in b_own]]
    pallas_call x3 -> x4, Pallas kernels: 9.05 us -> 9.05 us  [the longest x1 5.62 us: exchange_rows(): pl.pallas_call(exchange_kernel, in_specs=[SMEM, VMEM] + [VMEM] * len(piec...]
  transfers between devices with their start and end apart: 2 -> 6, of which waited for: 1 -> 2; matrix products, arithmetic and copies ran while one was open for 0% -> 0% of each run, Pallas kernels for 0% -> 1%
where the time goes in v3:
time: 91.4 us; the launch traced here: 90.6 us
  blocking collectives  47.7 us (52%)
  starting transfers between devices  24.9 us (27%)
  Pallas kernels  10.1 us (11%)
  local copies, waits for them, and re-layouts  4.91 us (5%)
  waiting for transfers between devices  2.9 us (3%)
    all_to_all x1, blocking collectives, per_device(): parts = lax.all_to_all(sum_xy(parts), ('z', 'c'), 0, 0, tiled=True)  24.9 us
    all_to_all x1, blocking collectives, per_device(): parts = lax.all_to_all(parts, ('x', 'y'), 0, 0, tiled=True)  22.8 us
    ppermute x4, starting transfers between devices, per_device(): b_other = [lax.ppermute(piece, 'c', swap) for piece in b_own]  15.1 us
    all_to_all x1, starting transfers between devices, per_device(): d_own = lax.all_to_all(mine, 'y', 0, 0, tiled=True)  7.65 us
    pallas_call x1, Pallas kernels, exchange_rows(): pl.pallas_call(exchange_kernel, in_specs=[SMEM, VMEM] + [VMEM] * len(piec...  5.62 us
    unnamed x16, local copies, waits for them, and re-layouts  4.91 us
    ppermute x1, starting transfers between devices, per_device(): d_other = lax.ppermute(d_own, 'c', swap)  2.16 us
  transfers between devices with their start and end apart: 6, of which 2 were waited for; matrix products, arithmetic and copies ran while one was open for 0% of the time, Pallas kernels for 1%

profile of v3, /device:TPU:1, one launch (start us, length us, event | category | flops | bytes accessed | tf_op | source)
XLA Modules:
  0.0 90.6 jit_solution(13870820080849178241)
XLA Ops:
  0.0 0.0 copy-start.7
  0.0 0.0 copy-start.5
  0.0 0.9 %copy-done.5 = bf16[96,768]{1,0:T(8,128)(2,1)S(1)} copy-done((bf16[96,768]{1,0:T(8,128)(2,1)S(1)}, bf16[96,768]{1,0:T(8,128)(2,1)}, u32[]{:S(2)}) %copy-start.5) | copy-done | bytes 147480
  0.9 0.8 pack.1
  1.7 7.7 %all-to-all-start = ((bf16[8,96,256]{2,1,0:T(8,128)(2,1)}), bf16[8,96,256]{2,1,0:T(8,128)(2,1)}, u32[]{:S(2)}, u32[]{:S(2)}) async-start(bf16[8,96,256]{2,1,0:T(8,128)(2,1)} %pack.1), calls=%async_computation | async-start | bytes 786432 | tf_op jit(solution)/shard_map/all_to_all | solution.py:214
  9.4 0.0 copy-start
  9.4 1.7 %copy-done = bf16[2,768,768]{2,1,0:T(8,128)(2,1)S(1)} copy-done((bf16[2,768,768]{2,1,0:T(8,128)(2,1)S(1)}, bf16[2,768,768]{2,1,0:T(8,128)(2,1)}, u32[]{:S(2)}) %copy-start) | copy-done | bytes 2359320
  11.1 0.0 copy-start.6
  11.1 0.7 copy-done.6
  11.8 1.2 %mask.1 = (bf16[24,16,768]{2,1,0:T(8,128)(2,1)S(1)}, bf16[24,16,768]{2,1,0:T(8,128)(2,1)S(1)}, bf16[24,16,768]{2,1,0:T(8,128)(2,1)S(1)}, bf16[24,16,768]{2,1,0:T(8,128)(2,1)S(1)}) custom-call(s32[6,2,6]{2,1,0:T(2,128)S(1)} %bitcast.6, bf16[2,48,16,768]{3,2,1,0:T(8,128)(2,1)S(1)} %bitcast.5), custom_call_target="tpu_custom_call" | custom-call | tf_op jit(solution)/shard_map/mask/pallas_call | solution.py:48
  12.9 8.9 %collective-permute-start = (bf16[24,16,768]{2,1,0:T(8,128)(2,1)S(1)}, bf16[24,16,768]{2,1,0:T(8,128)(2,1)S(1)}, u32[]{:S(2)}, u32[]{:S(2)}) collective-permute-start(bf16[24,16,768]{2,1,0:T(8,128)(2,1)S(1)} %get-tuple-element.18.refs_0_), channel_id=1, source_target_pairs={{0,8},{8,0},{1,9},{9,1},{2,10},{10,2},{3,11},{11,3},{4,12},{12,4},... | collective-permute-start | bytes 1769480 | tf_op jit(solution)/shard_map/ppermute | solution.py:213
  21.8 1.9 %collective-permute-start.1 = (bf16[24,16,768]{2,1,0:T(8,128)(2,1)S(1)}, bf16[24,16,768]{2,1,0:T(8,128)(2,1)S(1)}, u32[]{:S(2)}, u32[]{:S(2)}) collective-permute-start(bf16[24,16,768]{2,1,0:T(8,128)(2,1)S(1)} %get-tuple-element.19.refs_1_), channel_id=1, source_target_pairs={{0,8},{8,0},{1,9},{9,1},{2,10},{10,2},{3,11},{11,3},{4,12},{12,4},... | collective-permute-start | bytes 1769480 | tf_op jit(solution)/shard_map/ppermute | solution.py:213
  23.7 2.4 %collective-permute-start.2 = (bf16[24,16,768]{2,1,0:T(8,128)(2,1)S(1)}, bf16[24,16,768]{2,1,0:T(8,128)(2,1)S(1)}, u32[]{:S(2)}, u32[]{:S(2)}) collective-permute-start(bf16[24,16,768]{2,1,0:T(8,128)(2,1)S(1)} %get-tuple-element.20.refs_2_), channel_id=1, source_target_pairs={{0,8},{8,0},{1,9},{9,1},{2,10},{10,2},{3,11},{11,3},{4,12},{12,4},... | collective-permute-start | bytes 1769480 | tf_op jit(solution)/shard_map/ppermute | solution.py:213
  26.2 1.9 %collective-permute-start.3 = (bf16[24,16,768]{2,1,0:T(8,128)(2,1)S(1)}, bf16[24,16,768]{2,1,0:T(8,128)(2,1)S(1)}, u32[]{:S(2)}, u32[]{:S(2)}) collective-permute-start(bf16[24,16,768]{2,1,0:T(8,128)(2,1)S(1)} %get-tuple-element.21.refs_3_), channel_id=1, source_target_pairs={{0,8},{8,0},{1,9},{9,1},{2,10},{10,2},{3,11},{11,3},{4,12},{12,4},... | collective-permute-start | bytes 1769480 | tf_op jit(solution)/shard_map/ppermute | solution.py:213
  28.1 0.0 collective-permute-done.refs_4_
  28.1 0.0 collective-permute-done.1.refs_5_
  28.1 0.0 collective-permute-done.2.refs_6_
  28.1 0.0 copy-start.1
  28.1 0.8 copy-done.1
  28.9 1.1 %collective-permute-done.3.refs_7_ = bf16[24,16,768]{2,1,0:T(8,128)(2,1)S(1)} collective-permute-done((bf16[24,16,768]{2,1,0:T(8,128)(2,1)S(1)}, bf16[24,16,768]{2,1,0:T(8,128)(2,1)S(1)}, u32[]{:S(2)}, u32[]{:S(2)}) %collective-permute-start.3) | collective-permute-done | bytes 589856 | tf_op jit(solution)/shard_map/ppermute | solution.py:213
  30.1 0.0 copy-start.3
  30.1 0.8 copy-done.3
  30.9 0.0 all-to-all-done.d_own
  30.9 0.0 copy-start.2
  30.9 0.0 copy-start.4
  30.9 2.2 %collective-permute-start.4 = (bf16[8,96,256]{2,1,0:T(8,128)(2,1)}, bf16[8,96,256]{2,1,0:T(8,128)(2,1)S(1)}, u32[]{:S(2)}, u32[]{:S(2)}) collective-permute-start(bf16[8,96,256]{2,1,0:T(8,128)(2,1)} %all-to-all-done.d_own), channel_id=1, source_target_pairs={{0,8},{8,0},{1,9},{9,1},{2,10},{10,2},{3,11},{11,3},{4,12},{12,4},... | collective-permute-start | bytes 1179656 | tf_op jit(solution)/shard_map/ppermute | solution.py:216
  33.0 1.8 %collective-permute-done.4.d_other = bf16[8,96,256]{2,1,0:T(8,128)(2,1)S(1)} collective-permute-done((bf16[8,96,256]{2,1,0:T(8,128)(2,1)}, bf16[8,96,256]{2,1,0:T(8,128)(2,1)S(1)}, u32[]{:S(2)}, u32[]{:S(2)}) %collective-permute-start.4) | collective-permute-done | bytes 393248 | tf_op jit(solution)/shard_map/ppermute | solution.py:216
  34.8 0.0 copy-done.7
  34.8 1.4 %density.3.d = bf16[768,768]{1,0:T(8,128)(2,1)S(1)} custom-call(s32[1]{0:T(128)} %bitcast.core_ref, s32[6,6]{1,0:T(8,128)S(1)} %copy-done.7, bf16[8,96,256]{2,1,0:T(8,128)(2,1)} %all-to-all-done.d_own, bf16[8,96,256]{2,1,0:T(8,128)(2,1)S(1)} %collective-permute-done.4.d_other), custom_call_target="tpu_custom_call" | custom-call | flops 99999997952 | tf_op jit(solution)/shard_map/density/pallas_call | solution.py:79
  36.3 0.0 copy-done.2
  36.3 0.0 copy-done.4
  36.3 5.6 %exchange.1 = bf16[32,72,128]{2,1,0:T(8,128)(2,1)S(1)} custom-call(s32[1]{0:T(128)} %bitcast.core_ref, bf16[768,768]{1,0:T(8,128)(2,1)S(1)} %density.3.d, bf16[24,16,768]{2,1,0:T(8,128)(2,1)S(1)} %get-tuple-element.18.refs_0_, bf16[24,16,768]{2,1,0:T(8,128)(2,1)S(1)} %get-tuple-element.19.refs_1_, bf16[24,16,768]{2,1,0:T(8,128)(2,1)S(1)} %get-tuple-element.20.refs_2_, ...), custom_call_target="tpu_custom_call" | custom-call | tf_op jit(solution)/shard_map/exchange/pallas_call | solution.py:127
  41.9 22.8 %all_to_all.15.in_ref = bf16[32,72,128]{2,1,0:T(8,128)(2,1)S(1)} all-to-all(bf16[32,72,128]{2,1,0:T(8,128)(2,1)S(1)} %exchange.1), channel_id=1, replica_groups=mesh['z'=12,'x'=4,'c'=2,'y'=8] {'x','y'}, dimensions={0} | all-to-all | bytes 1179648 | tf_op jit(solution)/shard_map/all_to_all | solution.py:219
  64.7 0.3 sum_xy.1
  65.0 24.9 %all_to_all.16.in_ref = f32[24,4,128]{2,1,0:T(4,128)S(1)} all-to-all(f32[24,4,128]{2,1,0:T(4,128)S(1)} %sum_xy.1), channel_id=1, replica_groups=mesh['z'=12,'x'=4,'c'=2,'y'=8] {'z','c'}, dimensions={0} | all-to-all | bytes 98304 | tf_op jit(solution)/shard_map/all_to_all | solution.py:220
  89.9 0.7 sum_z.1
Async XLA Ops:
  0.0 34.8 %copy-start.7 = (s32[6,6]{1,0:T(8,128)S(1)}, s32[6,6]{1,0:T(8,128)}, u32[]{:S(2)}) copy-start(s32[6,6]{1,0:T(8,128)} %d_pattern.1) | copy-start | bytes 436
  0.0 0.9 %copy-start.5 = (bf16[96,768]{1,0:T(8,128)(2,1)S(1)}, bf16[96,768]{1,0:T(8,128)(2,1)}, u32[]{:S(2)}) copy-start(bf16[96,768]{1,0:T(8,128)(2,1)} %density.2) | copy-start | bytes 442372
  1.7 29.1 %all-to-all-start = ((bf16[8,96,256]{2,1,0:T(8,128)(2,1)}), bf16[8,96,256]{2,1,0:T(8,128)(2,1)}, u32[]{:S(2)}, u32[]{:S(2)}) async-start(bf16[8,96,256]{2,1,0:T(8,128)(2,1)} %pack.1), calls=%async_computation | async-start | bytes 786432 | tf_op jit(solution)/shard_map/all_to_all | solution.py:214
  9.4 1.7 %copy-start = (bf16[2,768,768]{2,1,0:T(8,128)(2,1)S(1)}, bf16[2,768,768]{2,1,0:T(8,128)(2,1)}, u32[]{:S(2)}) copy-start(bf16[2,768,768]{2,1,0:T(8,128)(2,1)} %param.4) | copy-start | bytes 7077892
  11.1 0.7 copy-start.6
  12.9 15.2 %collective-permute-start = (bf16[24,16,768]{2,1,0:T(8,128)(2,1)S(1)}, bf16[24,16,768]{2,1,0:T(8,128)(2,1)S(1)}, u32[]{:S(2)}, u32[]{:S(2)}) collective-permute-start(bf16[24,16,768]{2,1,0:T(8,128)(2,1)S(1)} %get-tuple-element.18.refs_0_), channel_id=1, source_target_pairs={{0,8},{8,0},{1,9},{9,1},{2,10},{10,2},{3,11},{11,3},{4,12},{12,4},... | collective-permute-start | bytes 1769480 | tf_op jit(solution)/shard_map/ppermute | solution.py:213
  21.8 6.3 %collective-permute-start.1 = (bf16[24,16,768]{2,1,0:T(8,128)(2,1)S(1)}, bf16[24,16,768]{2,1,0:T(8,128)(2,1)S(1)}, u32[]{:S(2)}, u32[]{:S(2)}) collective-permute-start(bf16[24,16,768]{2,1,0:T(8,128)(2,1)S(1)} %get-tuple-element.19.refs_1_), channel_id=1, source_target_pairs={{0,8},{8,0},{1,9},{9,1},{2,10},{10,2},{3,11},{11,3},{4,12},{12,4},... | collective-permute-start | bytes 1769480 | tf_op jit(solution)/shard_map/ppermute | solution.py:213
  23.7 4.4 %collective-permute-start.2 = (bf16[24,16,768]{2,1,0:T(8,128)(2,1)S(1)}, bf16[24,16,768]{2,1,0:T(8,128)(2,1)S(1)}, u32[]{:S(2)}, u32[]{:S(2)}) collective-permute-start(bf16[24,16,768]{2,1,0:T(8,128)(2,1)S(1)} %get-tuple-element.20.refs_2_), channel_id=1, source_target_pairs={{0,8},{8,0},{1,9},{9,1},{2,10},{10,2},{3,11},{11,3},{4,12},{12,4},... | collective-permute-start | bytes 1769480 | tf_op jit(solution)/shard_map/ppermute | solution.py:213
  26.2 3.9 %collective-permute-start.3 = (bf16[24,16,768]{2,1,0:T(8,128)(2,1)S(1)}, bf16[24,16,768]{2,1,0:T(8,128)(2,1)S(1)}, u32[]{:S(2)}, u32[]{:S(2)}) collective-permute-start(bf16[24,16,768]{2,1,0:T(8,128)(2,1)S(1)} %get-tuple-element.21.refs_3_), channel_id=1, source_target_pairs={{0,8},{8,0},{1,9},{9,1},{2,10},{10,2},{3,11},{11,3},{4,12},{12,4},... | collective-permute-start | bytes 1769480 | tf_op jit(solution)/shard_map/ppermute | solution.py:213
  28.1 0.8 copy-start.1
  30.1 0.8 copy-start.3
  30.9 5.4 %copy-start.2 = (bf16[24,16,768]{2,1,0:T(8,128)(2,1)S(1)}, bf16[24,16,768]{2,1,0:T(8,128)(2,1)}, u32[]{:S(2)}) copy-start(bf16[24,16,768]{2,1,0:T(8,128)(2,1)} %copy-done.1) | copy-start | bytes 1769476
  30.9 5.4 %copy-start.4 = (bf16[24,16,768]{2,1,0:T(8,128)(2,1)S(1)}, bf16[24,16,768]{2,1,0:T(8,128)(2,1)}, u32[]{:S(2)}) copy-start(bf16[24,16,768]{2,1,0:T(8,128)(2,1)} %copy-done.3) | copy-start | bytes 1769476
  30.9 3.9 %collective-permute-start.4 = (bf16[8,96,256]{2,1,0:T(8,128)(2,1)}, bf16[8,96,256]{2,1,0:T(8,128)(2,1)S(1)}, u32[]{:S(2)}, u32[]{:S(2)}) collective-permute-start(bf16[8,96,256]{2,1,0:T(8,128)(2,1)} %all-to-all-done.d_own), channel_id=1, source_target_pairs={{0,8},{8,0},{1,9},{9,1},{2,10},{10,2},{3,11},{11,3},{4,12},{12,4},... | collective-permute-start | bytes 1179656 | tf_op jit(solution)/shard_map/ppermute | solution.py:216

commit v4 on v2

--- a/solution.py
+++ b/solution.py
@@ -19,9 +19,19 @@
 SENT = 4
 PACK = ROWS * Z * G // 128
 MAIN = 128 // G
+COST = 10**11
+MIB = 1024 * 1024
 VMEM = pl.BlockSpec(memory_space=pltpu.VMEM)
 SMEM = pl.BlockSpec(memory_space=pltpu.SMEM)
 ANY = pl.BlockSpec(memory_space=pl.ANY)
+
+
+def hbm(x):
+    return pltpu.with_memory_space_constraint(x, pltpu.HBM)
+
+
+def vmem(x):
+    return pltpu.with_memory_space_constraint(x, pltpu.VMEM)
 
 
 def place(z, x):
@@ -48,11 +58,40 @@
         in_specs=[SMEM, spec],
         out_specs=spec,
         out_shape=pltpu.VMEM((count, GROUPS, G, A), jnp.bfloat16),
+        cost_estimate=pl.CostEstimate(flops=COST, bytes_accessed=0, transcendentals=0),
+        compiler_params=pltpu.CompilerParams(vmem_limit_bytes=16 * MIB),
         name="mask",
-    )(b_pattern.transpose(1, 0, 2), three_center.reshape(count, GROUPS, G, A))
-
-
-def exchange_kernel(count, core_ref, d_pattern, d_own, d_other, b_own, b_other, out_ref, d, acc):
+    )(hbm(b_pattern.transpose(1, 0, 2)), hbm(three_center.reshape(count, GROUPS, G, A)))
+
+
+def density_mask_kernel(core_ref, d_pattern, part, out_ref):
+    core = core_ref[0]
+    for y in range(Y):
+        for t in range(YROWS // STEP):
+            rb = (y * YROWS + t * STEP) // BS
+            here = slice(t * STEP, (t + 1) * STEP)
+            for j in range(SENT // C):
+                col = lax.rem(rb + core * (SENT // C) + j, NB)
+                keep = jnp.maximum(d_pattern[rb, col], d_pattern[col, rb]) > 0
+                block = part[y, here, j * BS : (j + 1) * BS]
+                out_ref[y, here, j * BS : (j + 1) * BS] = jnp.where(keep, block, jnp.zeros_like(block))
+
+
+def mask_density(core, d_pattern, part):
+    return pl.pallas_call(
+        density_mask_kernel,
+        in_specs=[SMEM, SMEM, VMEM],
+        out_specs=VMEM,
+        out_shape=pltpu.VMEM(part.shape, jnp.bfloat16),
+        cost_estimate=pl.CostEstimate(flops=COST, bytes_accessed=0, transcendentals=0),
+        compiler_params=pltpu.CompilerParams(vmem_limit_bytes=8 * MIB),
+        name="density_mask",
+    )(core, hbm(d_pattern), vmem(part))
+
+
+def exchange_kernel(count, core_ref, d_own, d_other, b_own, b_there, out_ref, d, acc, b_other, arrived):
+    fetch = pltpu.make_async_copy(b_there, b_other, arrived)
+    fetch.start()
     core = core_ref[0]
     for h, part in ((core, d_own), (1 - core, d_other)):
         for y in range(Y):
@@ -61,16 +100,16 @@
                 here = slice(y * YROWS + t * STEP, y * YROWS + (t + 1) * STEP)
                 for j in range(SENT // C):
                     col = lax.rem(rb + h * (SENT // C) + j, NB)
-                    keep = jnp.maximum(d_pattern[rb, col], d_pattern[col, rb]) > 0
-                    block = part[y, t * STEP : (t + 1) * STEP, j * BS : (j + 1) * BS]
                     lanes = pl.ds(pl.multiple_of(col * BS, BS), BS)
-                    d[here, lanes] = jnp.where(keep, block, jnp.zeros_like(block))
+                    d[here, lanes] = part[y, t * STEP : (t + 1) * STEP, j * BS : (j + 1) * BS]
     for rb in range(NB):
         for k in range(SENT, NB):
             cb = (rb + k) % NB
             rows, cols = slice(rb * BS, (rb + 1) * BS), slice(cb * BS, (cb + 1) * BS)
             d[rows, cols] = d[cols, rows].T
     for p in range(2 * count):
+        if p == count:
+            fetch.wait()
         b = b_own.at[p] if p < count else b_other.at[p - count]
         full = b[...].reshape(A, A)
         for q in range(X // 2):
@@ -100,24 +139,26 @@
             out_ref[(2 * q + 1) * Y + y] = jnp.concatenate([last, odd], 0).astype(jnp.bfloat16)
 
 
-def exchange_rows(core, d_pattern, d_own, d_other, b_own, b_other):
+def exchange_rows(core, d_own, d_other, b_own, b_other):
     count = b_own.shape[0]
     return pl.pallas_call(
         functools.partial(exchange_kernel, count),
-        in_specs=[SMEM, SMEM, VMEM, VMEM, VMEM, VMEM],
+        in_specs=[SMEM, VMEM, VMEM, VMEM, ANY],
         out_specs=VMEM,
         out_shape=pltpu.VMEM((X * Y, PACK, 128), jnp.bfloat16),
         scratch_shapes=[
             pltpu.VMEM((A, A), jnp.bfloat16),
             pltpu.VMEM((Y * ROWS, A), jnp.float32),
+            pltpu.VMEM(b_other.shape, jnp.bfloat16),
+            pltpu.SemaphoreType.DMA,
         ],
-        compiler_params=pltpu.CompilerParams(vmem_limit_bytes=40 * 1024 * 1024),
+        compiler_params=pltpu.CompilerParams(vmem_limit_bytes=24 * MIB),
         name="exchange",
-    )(core, d_pattern, d_own, d_other, b_own, pltpu.with_memory_space_constraint(b_other, pltpu.VMEM))
-
-
-def pack_kernel(place_ref, density, out_ref):
-    y, core = place_ref[0], place_ref[1]
+    )(core, vmem(d_own), vmem(d_other), vmem(b_own), b_other)
+
+
+def pack_kernel(y_ref, core_ref, density, out_ref):
+    y, core = y_ref[0], core_ref[0]
     for t in range(YROWS // STEP):
         rb = lax.div(y * YROWS + t * STEP, BS)
         for j in range(SENT // C):
@@ -127,14 +168,15 @@
                 out_ref[to, t * STEP : (t + 1) * STEP, j * BS : (j + 1) * BS] = block
 
 
-def pack_density(place_at, density):
+def pack_density(y, core, density):
     return pl.pallas_call(
         pack_kernel,
-        in_specs=[SMEM, VMEM],
+        in_specs=[SMEM, SMEM, VMEM],
         out_specs=VMEM,
         out_shape=pltpu.VMEM((Y, YROWS, SENT // C * BS), jnp.bfloat16),
+        compiler_params=pltpu.CompilerParams(vmem_limit_bytes=8 * MIB),
         name="pack",
-    )(place_at, density)
+    )(y, core, hbm(density))
 
 
 def sum_xy_kernel(in_ref, out_ref):
@@ -146,8 +188,9 @@
     rest = rest.T
     rest = jnp.concatenate([rest[:64], rest[64:]], 1)
     both = jnp.concatenate([first, rest], 0)
-    both = jnp.concatenate([both, jnp.zeros((Z * G, 128 - ROWS), jnp.float32)], 1)
-    out_ref[...] = both.reshape(Z * C, K, 128)
+    both = both.reshape(Z * C, K, ROWS)
+    pad = jnp.zeros((Z * C, K // 2, 128 - 2 * ROWS), jnp.float32)
+    out_ref[...] = jnp.concatenate([both[:, : K // 2], both[:, K // 2 :], pad], 2)
 
 
 def sum_xy(parts):
@@ -155,9 +198,10 @@
         sum_xy_kernel,
         in_specs=[VMEM],
         out_specs=VMEM,
-        out_shape=pltpu.VMEM((Z * C, K, 128), jnp.float32),
+        out_shape=pltpu.VMEM((Z * C, K // 2, 128), jnp.float32),
+        compiler_params=pltpu.CompilerParams(vmem_limit_bytes=8 * MIB),
         name="sum_xy",
-    )(pltpu.with_memory_space_constraint(parts, pltpu.VMEM))
+    )(vmem(parts))
 
 
 def sum_z_kernel(factor, in_ref, out_ref):
@@ -166,6 +210,7 @@
         total = in_ref[c]
         for z in range(1, Z):
             total = total + in_ref[z * C + c]
+        total = jnp.concatenate([total[:, :ROWS], total[:, ROWS : 2 * ROWS]], 0)
         halves.append(total * factor)
     out_ref[...] = jnp.concatenate([halves[g % C][:, g // C * G : (g // C + 1) * G] for g in range(YROWS // G)], 1)
 
@@ -176,20 +221,22 @@
         in_specs=[VMEM],
         out_specs=VMEM,
         out_shape=jax.ShapeDtypeStruct((K, YROWS), jnp.float32),
+        compiler_params=pltpu.CompilerParams(vmem_limit_bytes=4 * MIB),
         name="sum_z",
-    )(pltpu.with_memory_space_constraint(parts, pltpu.VMEM))
+    )(vmem(parts))
 
 
 def per_device(three_center, b_pattern, density, d_pattern):
-    core, y = lax.axis_index("c"), lax.axis_index("y")
+    core, y = lax.axis_index("c").reshape(1), lax.axis_index("y").reshape(1)
     swap = [(0, 1), (1, 0)]
-    mine = pack_density(jnp.stack([y, core]), density)
+    mine = pack_density(y, core, density)
     mine, b_pattern = lax.optimization_barrier((mine, b_pattern))
     b_own = mask_and_order(three_center, b_pattern)
     b_other = lax.ppermute(b_own, "c", swap)
-    d_own = lax.all_to_all(mine, "y", 0, 0, tiled=True)
+    d_own = mask_density(core, d_pattern, lax.all_to_all(mine, "y", 0, 0, tiled=True))
+    d_own, b_other = lax.optimization_barrier((d_own, b_other))
     d_other = lax.ppermute(d_own, "c", swap)
-    parts = exchange_rows(core.reshape(1), d_pattern, d_own, d_other, b_own, b_other)
+    parts = exchange_rows(core, d_own, d_other, b_own, b_other)
     parts = lax.all_to_all(parts, ("x", "y"), 0, 0, tiled=True)
     parts = lax.all_to_all(sum_xy(parts), ("z", "c"), 0, 0, tiled=True)
     total_ri = three_center.shape[0] * Z * X * C * Y

time: 89.4 us -> 84.8 us (0.949)
  blocking collectives: 62 us -> 45.8 us
  starting transfers between devices: 14.8 us -> 22.3 us
  waiting for transfers between devices: 1.33 us -> 4.73 us
  Pallas kernels: 9.93 us -> 11.1 us
    all_to_all x1 -> x0, blocking collectives: 17.6 us -> none  [per_device(): d_own = lax.all_to_all(mine, 'y', 0, 0, tiled=True)]
    all_to_all x0 -> x1, starting transfers between devices: none -> 7.65 us  [per_device(): lax.all_to_all(mine, 'y', 0, 0, tiled=True)]
    ppermute x1, starting transfers between devices: 12.4 us -> 8.24 us  [per_device(): b_other = lax.ppermute(b_own, 'c', swap)]
    ppermute x1, starting transfers between devices: 2.34 us -> 6.44 us  [per_device(): d_other = lax.ppermute(d_own, 'c', swap)]
    ppermute x1, waiting for transfers between devices: 0.01 us -> 2.84 us  [per_device(): b_other = lax.ppermute(b_own, 'c', swap)]
    pallas_call x1 -> x2, Pallas kernels: 0.99 us -> 2.57 us  [the longest x1 1.71 us: pack_density(): pl.pallas_call(pack_kernel, in_specs=[SMEM, SMEM, VMEM], out_specs=VMEM,...]
    all_to_all x1, blocking collectives: 25.6 us -> 26.9 us  [per_device(): parts = lax.all_to_all(sum_xy(parts), ('z', 'c'), 0, 0, tiled=True)]
  transfers between devices with their start and end apart: 2 -> 3, of which waited for: 1 -> 3; matrix products, arithmetic and copies ran while one was open for 0% -> 0% of each run, Pallas kernels for 0% -> 3%
where the time goes in v4:
time: 84.8 us; the launch traced here: 84 us
  blocking collectives  45.8 us (54%)
  starting transfers between devices  22.3 us (26%)
  Pallas kernels  11.1 us (13%)
  waiting for transfers between devices  4.73 us (6%)
    all_to_all x1, blocking collectives, per_device(): parts = lax.all_to_all(sum_xy(parts), ('z', 'c'), 0, 0, tiled=True)  26.9 us
    all_to_all x1, blocking collectives, per_device(): parts = lax.all_to_all(parts, ('x', 'y'), 0, 0, tiled=True)  18.8 us
    ppermute x1, starting transfers between devices, per_device(): b_other = lax.ppermute(b_own, 'c', swap)  8.24 us
    all_to_all x1, starting transfers between devices, per_device(): lax.all_to_all(mine, 'y', 0, 0, tiled=True)  7.65 us
    ppermute x1, starting transfers between devices, per_device(): d_other = lax.ppermute(d_own, 'c', swap)  6.44 us
    pallas_call x1, Pallas kernels, exchange_rows(): pl.pallas_call(functools.partial(exchange_kernel, count), in_specs=[SMEM,...  5.61 us
    ppermute x1, waiting for transfers between devices, per_device(): b_other = lax.ppermute(b_own, 'c', swap)  2.84 us
    pallas_call x1, Pallas kernels, mask_and_order(): pl.pallas_call(mask_kernel, grid=(count,), in_specs=[SMEM, spec], out_spe...  1.94 us
  transfers between devices with their start and end apart: 3, of which 3 were waited for; matrix products, arithmetic and copies ran while one was open for 0% of the time, Pallas kernels for 3%

profile of v4, /device:TPU:1, one launch (start us, length us, event | category | flops | bytes accessed | tf_op | source)
XLA Modules:
  0.0 84.0 jit_solution(4488226226639298260)
XLA Ops:
  0.0 1.7 %pack.1 = bf16[8,96,256]{2,1,0:T(8,128)(2,1)} custom-call(s32[1]{0:T(128)} %bitcast.1.y_ref, s32[1]{0:T(128)} %bitcast.core_ref, bf16[96,768]{1,0:T(8,128)(2,1)} %density.1), custom_call_target="tpu_custom_call" | custom-call | tf_op jit(solution)/shard_map/pack/pallas_call | solution.py:172
  1.7 7.7 %all-to-all-start = ((bf16[8,96,256]{2,1,0:T(8,128)(2,1)}), bf16[8,96,256]{2,1,0:T(8,128)(2,1)S(1)}, u32[]{:S(2)}, u32[]{:S(2)}) async-start(bf16[8,96,256]{2,1,0:T(8,128)(2,1)} %pack.1), calls=%async_computation | async-start | bytes 786432 | tf_op jit(solution)/shard_map/all_to_all | solution.py:236
  9.4 1.9 %mask.1.b_own = bf16[2,48,16,768]{3,2,1,0:T(8,128)(2,1)S(1)} custom-call(s32[6,2,6]{2,1,0:T(2,128)} %bitcast.6, bf16[2,48,16,768]{3,2,1,0:T(8,128)(2,1)} %bitcast.5), custom_call_target="tpu_custom_call" | custom-call | flops 99999997952 | tf_op jit(solution)/shard_map/mask/pallas_call | solution.py:55
  11.3 8.2 %collective-permute-start = (bf16[2,48,16,768]{3,2,1,0:T(8,128)(2,1)S(1)}, bf16[2,48,16,768]{3,2,1,0:T(8,128)(2,1)}, u32[]{:S(2)}, u32[]{:S(2)}) collective-permute-start(bf16[2,48,16,768]{3,2,1,0:T(8,128)(2,1)S(1)} %mask.1.b_own), channel_id=1, source_target_pairs={{0,8},{8,0},{1,9},{9,1},{2,10},{10,2},{3,11},{11,3},{4,12},{12,4},... | collective-permute-start | bytes 7077896 | tf_op jit(solution)/shard_map/ppermute | solution.py:235
  19.6 0.6 all-to-all-done.part
  20.1 0.9 %density_mask.1.d_own = bf16[8,96,256]{2,1,0:T(8,128)(2,1)S(1)} custom-call(s32[1]{0:T(128)} %bitcast.core_ref, s32[6,6]{1,0:T(8,128)} %d_pattern.1, bf16[8,96,256]{2,1,0:T(8,128)(2,1)S(1)} %all-to-all-done.part), custom_call_target="tpu_custom_call" | custom-call | flops 99999997952 | tf_op jit(solution)/shard_map/density_mask/pallas_call | solution.py:81
  21.0 2.8 %collective-permute-done.b_there = bf16[2,48,16,768]{3,2,1,0:T(8,128)(2,1)} collective-permute-done((bf16[2,48,16,768]{3,2,1,0:T(8,128)(2,1)S(1)}, bf16[2,48,16,768]{3,2,1,0:T(8,128)(2,1)}, u32[]{:S(2)}, u32[]{:S(2)}) %collective-permute-start) | collective-permute-done | bytes 2359328 | tf_op jit(solution)/shard_map/ppermute | solution.py:235
  23.8 6.4 %collective-permute-start.1 = (bf16[8,96,256]{2,1,0:T(8,128)(2,1)S(1)}, bf16[8,96,256]{2,1,0:T(8,128)(2,1)S(1)}, u32[]{:S(2)}, u32[]{:S(2)}) collective-permute-start(bf16[8,96,256]{2,1,0:T(8,128)(2,1)S(1)} %density_mask.1.d_own), channel_id=1, source_target_pairs={{0,8},{8,0},{1,9},{9,1},{2,10},{10,2},{3,11},{11,3},{4,12},{12,4},... | collective-permute-start | bytes 1179656 | tf_op jit(solution)/shard_map/ppermute | solution.py:238
  30.3 1.3 %collective-permute-done.1.d_other = bf16[8,96,256]{2,1,0:T(8,128)(2,1)S(1)} collective-permute-done((bf16[8,96,256]{2,1,0:T(8,128)(2,1)S(1)}, bf16[8,96,256]{2,1,0:T(8,128)(2,1)S(1)}, u32[]{:S(2)}, u32[]{:S(2)}) %collective-permute-start.1) | collective-permute-done | bytes 393248 | tf_op jit(solution)/shard_map/ppermute | solution.py:238
  31.6 5.6 %exchange.1 = bf16[32,72,128]{2,1,0:T(8,128)(2,1)S(1)} custom-call(s32[1]{0:T(128)} %bitcast.core_ref, bf16[8,96,256]{2,1,0:T(8,128)(2,1)S(1)} %density_mask.1.d_own, bf16[8,96,256]{2,1,0:T(8,128)(2,1)S(1)} %collective-permute-done.1.d_other, bf16[2,48,16,768]{3,2,1,0:T(8,128)(2,1)S(1)} %mask.1.b_own, bf16[2,48,16,768]{3,2,1,0:T(8,128)(2,1)} %collective-permute-done.b_there), custom_call_target="tpu_custom_call" | custom-call | tf_op jit(solution)/shard_map/exchange/pallas_call | solution.py:144
  37.2 18.8 %all_to_all.15.in_ref = bf16[32,72,128]{2,1,0:T(8,128)(2,1)S(1)} all-to-all(bf16[32,72,128]{2,1,0:T(8,128)(2,1)S(1)} %exchange.1), channel_id=1, replica_groups=mesh['z'=12,'x'=4,'c'=2,'y'=8] {'x','y'}, dimensions={0} | all-to-all | bytes 1179648 | tf_op jit(solution)/shard_map/all_to_all | solution.py:240
  56.0 0.3 sum_xy.1
  56.3 26.9 %all_to_all.16.in_ref = f32[24,4,128]{2,1,0:T(4,128)S(1)} all-to-all(f32[24,4,128]{2,1,0:T(4,128)S(1)} %sum_xy.1), channel_id=1, replica_groups=mesh['z'=12,'x'=4,'c'=2,'y'=8] {'z','c'}, dimensions={0} | all-to-all | bytes 98304 | tf_op jit(solution)/shard_map/all_to_all | solution.py:241
  83.3 0.7 sum_z.1
Async XLA Ops:
  1.7 18.4 %all-to-all-start = ((bf16[8,96,256]{2,1,0:T(8,128)(2,1)}), bf16[8,96,256]{2,1,0:T(8,128)(2,1)S(1)}, u32[]{:S(2)}, u32[]{:S(2)}) async-start(bf16[8,96,256]{2,1,0:T(8,128)(2,1)} %pack.1), calls=%async_computation | async-start | bytes 786432 | tf_op jit(solution)/shard_map/all_to_all | solution.py:236
  11.3 12.5 %collective-permute-start = (bf16[2,48,16,768]{3,2,1,0:T(8,128)(2,1)S(1)}, bf16[2,48,16,768]{3,2,1,0:T(8,128)(2,1)}, u32[]{:S(2)}, u32[]{:S(2)}) collective-permute-start(bf16[2,48,16,768]{3,2,1,0:T(8,128)(2,1)S(1)} %mask.1.b_own), channel_id=1, source_target_pairs={{0,8},{8,0},{1,9},{9,1},{2,10},{10,2},{3,11},{11,3},{4,12},{12,4},... | collective-permute-start | bytes 7077896 | tf_op jit(solution)/shard_map/ppermute | solution.py:235
  23.8 7.8 %collective-permute-start.1 = (bf16[8,96,256]{2,1,0:T(8,128)(2,1)S(1)}, bf16[8,96,256]{2,1,0:T(8,128)(2,1)S(1)}, u32[]{:S(2)}, u32[]{:S(2)}) collective-permute-start(bf16[8,96,256]{2,1,0:T(8,128)(2,1)S(1)} %density_mask.1.d_own), channel_id=1, source_target_pairs={{0,8},{8,0},{1,9},{9,1},{2,10},{10,2},{3,11},{11,3},{4,12},{12,4},... | collective-permute-start | bytes 1179656 | tf_op jit(solution)/shard_map/ppermute | solution.py:238

commit v5 on v4

v5 whole, which is shorter than its diff:
```python
import functools
import math

import jax
import jax.numpy as jnp
from jax import lax
from jax.experimental import pallas as pl
from jax.experimental.pallas import tpu as pltpu
from jax.sharding import Mesh, PartitionSpec as P

Z, X, C, Y = 12, 4, 2, 8
A, BS, NB = 768, 128, 6
K = 8
G = 16
GROUPS = A // G
ROWS = A // (Y * C)
YROWS = A // Y
STEP = 32
SENT = 4
PACK = ROWS * Z * G // 128
MAIN = 128 // G
COST = 10**11
MIB = 1024 * 1024
VMEM = pl.BlockSpec(memory_space=pltpu.VMEM)
SMEM = pl.BlockSpec(memory_space=pltpu.SMEM)
ANY = pl.BlockSpec(memory_space=pl.ANY)


def hbm(x):
    return pltpu.with_memory_space_constraint(x, pltpu.HBM)


def vmem(x):
    return pltpu.with_memory_space_constraint(x, pltpu.VMEM)


def place(z, x):
    return x * Z + z


def mask_kernel(pattern, b_ref, out_ref):
    p = pl.program_id(0)
    for rb in range(NB):
        for cb in range(NB):
            keep = pattern[rb, p, cb] > 0
            lanes = slice(cb * BS, (cb + 1) * BS)
            for g in range(rb * 8, rb * 8 + 8):
                block = b_ref[0, g, :, lanes]
                out_ref[0, place(g // X, g % X), :, lanes] = jnp.where(keep, block, jnp.zeros_like(block))


def mask_and_order(three_center, b_pattern):
    count = three_center.shape[0]
    spec = pl.BlockSpec((1, GROUPS, G, A), lambda p: (p, 0, 0, 0))
    return pl.pallas_call(
        mask_kernel,
        grid=(count,),
        in_specs=[SMEM, spec],
        out_specs=spec,
        out_shape=pltpu.VMEM((count, GROUPS, G, A), jnp.bfloat16),
        cost_estimate=pl.CostEstimate(flops=COST, bytes_accessed=0, transcendentals=0),
        compiler_params=pltpu.CompilerParams(vmem_limit_bytes=16 * MIB),
        name="mask",
    )(hbm(b_pattern.transpose(1, 0, 2)), hbm(three_center.reshape(count, GROUPS, G, A)))


def settle(part):
    return pl.pallas_call(
        lambda in_ref, out_ref: None,
        in_specs=[ANY],
        out_specs=ANY,
        out_shape=jax.ShapeDtypeStruct(part.shape, part.dtype),
        input_output_aliases={0: 0},
        cost_estimate=pl.CostEstimate(flops=COST, bytes_accessed=0, transcendentals=0),
        compiler_params=pltpu.CompilerParams(vmem_limit_bytes=MIB),
        name="settle",
    )(part)


def exchange_kernel(count, d_own, d_other, b_own, b_there, out_ref, d, acc, b_other, arrived):
    fetch = pltpu.make_async_copy(b_there, b_other, arrived)
    fetch.start()
    core = lax.axis_index("c")
    for h, part in ((core, d_own), (1 - core, d_other)):
        for y in range(Y):
            for t in range(YROWS // STEP):
                rb = (y * YROWS + t * STEP) // BS
                here = slice(y * YROWS + t * STEP, y * YROWS + (t + 1) * STEP)
                for j in range(SENT // C):
                    col = lax.rem(rb + h * (SENT // C) + j, NB)
                    lanes = pl.ds(pl.multiple_of(col * BS, BS), BS)
                    d[here, lanes] = part[y, t * STEP : (t + 1) * STEP, j * BS : (j + 1) * BS]
    for rb in range(NB):
        for k in range(SENT, NB):
            cb = (rb + k) % NB
            rows, cols = slice(rb * BS, (rb + 1) * BS), slice(cb * BS, (cb + 1) * BS)
            d[rows, cols] = d[cols, rows].T
    lane = lax.broadcasted_iota(jnp.int32, (ROWS // 2, 128), 1)
    top, bottom = slice(0, ROWS // 2), slice(ROWS // 2, ROWS)
    half_rows, halves = Z * G, X // 2
    for p in range(2 * count):
        if p == count:
            fetch.wait()
        b = b_own.at[p] if p < count else b_other.at[p - count]
        rows = [b[pl.ds((2 * q + core) * Z, Z)].reshape(half_rows, A) for q in range(halves)]
        half = jnp.dot(jnp.concatenate(rows, 0), d[...], preferred_element_type=jnp.float32).astype(jnp.bfloat16)
        for q in range(halves):
            full = b[q * 2 * Z : (q + 1) * 2 * Z].reshape(2 * half_rows, A)
            term = lax.dot_general(half, full, (((1,), (1,)), ((), ())), preferred_element_type=jnp.float32)
            cols = slice(q * 2 * half_rows, (q + 1) * 2 * half_rows)
            total = term if p == 0 else acc[:, cols] + term
            if p < 2 * count - 1:
                acc[:, cols] = total
                continue
            for y in range(Y):
                groups = []
                for t in range(ROWS // G):
                    z, x = divmod(y * (YROWS // G) + 2 * t, X)
                    at = (x // 2) * half_rows + z * G
                    groups.append(total[at : at + G])
                block = jnp.concatenate(groups, 0)
                first, middle, last = block[:, :128], block[:, 128:256], block[:, 256:]
                turned = pltpu.roll(middle, 64, 1)
                even = jnp.where(lane < 64, middle[top], turned[bottom])
                odd = jnp.where(lane < 64, turned[top], middle[bottom])
                out_ref[(2 * q) * Y + y] = jnp.concatenate([first, even], 0).astype(jnp.bfloat16)
                out_ref[(2 * q + 1) * Y + y] = jnp.concatenate([last, odd], 0).astype(jnp.bfloat16)


def exchange_rows(d_own, d_other, b_own, b_other):
    count = b_own.shape[0]
    return pl.pallas_call(
        functools.partial(exchange_kernel, count),
        in_specs=[VMEM, VMEM, VMEM, ANY],
        out_specs=VMEM,
        out_shape=pltpu.VMEM((X * Y, PACK, 128), jnp.bfloat16),
        scratch_shapes=[
            pltpu.VMEM((A, A), jnp.bfloat16),
            pltpu.VMEM((Y * ROWS, A), jnp.float32),
            pltpu.VMEM(b_other.shape, jnp.bfloat16),
            pltpu.SemaphoreType.DMA,
        ],
        compiler_params=pltpu.CompilerParams(vmem_limit_bytes=24 * MIB),
        name="exchange",
    )(vmem(d_own), vmem(d_other), vmem(b_own), b_other)


def pack_kernel(d_pattern, density, out_ref):
    y, core = lax.axis_index("y"), lax.axis_index("c")
    for t in range(YROWS // STEP):
        rb = lax.div(y * YROWS + t * STEP, BS)
        for j in range(SENT // C):
            col = lax.rem(rb + core * (SENT // C) + j, NB)
            keep = jnp.maximum(d_pattern[rb, col], d_pattern[col, rb]) > 0
            block = density[t * STEP : (t + 1) * STEP, pl.ds(pl.multiple_of(col * BS, BS), BS)]
            block = jnp.where(keep, block, jnp.zeros_like(block))
            for to in range(Y):
                out_ref[to, t * STEP : (t + 1) * STEP, j * BS : (j + 1) * BS] = block


def pack_density(d_pattern, density):
    return pl.pallas_call(
        pack_kernel,
        in_specs=[SMEM, VMEM],
        out_specs=VMEM,
        out_shape=pltpu.VMEM((Y, YROWS, SENT // C * BS), jnp.bfloat16),
        compiler_params=pltpu.CompilerParams(vmem_limit_bytes=8 * MIB),
        name="pack",
    )(hbm(d_pattern), hbm(density))


def sum_xy_kernel(in_ref, out_ref):
    total = in_ref[0].astype(jnp.float32)
    for i in range(1, X * Y):
        total = total + in_ref[i].astype(jnp.float32)
    first, rest = total[:ROWS].T, total[ROWS:].T
    rest = jnp.concatenate([rest[:64], rest[64:]], 1)
    odd = lax.rem(lax.axis_index("x"), 2)
    for part, at in ((first, odd * (Z - MAIN) * C), (rest, (1 - odd) * MAIN * C)):
        count = part.shape[0] // K
        part = part.reshape(count, K, ROWS)
        pad = jnp.zeros((count, K // 2, 128 - 2 * ROWS), jnp.float32)
        out_ref[pl.ds(at, count)] = jnp.concatenate([part[:, : K // 2], part[:, K // 2 :], pad], 2)


def sum_xy(parts):
    return pl.pallas_call(
        sum_xy_kernel,
        in_specs=[VMEM],
        out_specs=VMEM,
        out_shape=pltpu.VMEM((Z * C, K // 2, 128), jnp.float32),
        compiler_params=pltpu.CompilerParams(vmem_limit_bytes=8 * MIB),
        name="sum_xy",
    )(vmem(parts))


def sum_z_kernel(factor, in_ref, out_ref):
    halves = []
    for c in range(C):
        total = in_ref[c]
        for z in range(1, Z):
            total = total + in_ref[z * C + c]
        total = jnp.concatenate([total[:, :ROWS], total[:, ROWS : 2 * ROWS]], 0)
        halves.append(total * factor)
    out_ref[...] = jnp.concatenate([halves[g % C][:, g // C * G : (g // C + 1) * G] for g in range(YROWS // G)], 1)


def sum_z(parts, factor):
    return pl.pallas_call(
        functools.partial(sum_z_kernel, factor),
        in_specs=[VMEM],
        out_specs=VMEM,
        out_shape=jax.ShapeDtypeStruct((K, YROWS), jnp.float32),
        compiler_params=pltpu.CompilerParams(vmem_limit_bytes=4 * MIB),
        name="sum_z",
    )(vmem(parts))


def per_device(three_center, b_pattern, density, d_pattern):
    swap = [(0, 1), (1, 0)]
    mine = pack_density(d_pattern, density)
    mine, b_pattern = lax.optimization_barrier((mine, b_pattern))
    b_own = mask_and_order(three_center, b_pattern)
    b_other = lax.ppermute(b_own, "c", swap)
    d_own = settle(lax.all_to_all(mine, "y", 0, 0, tiled=True))
    d_own, b_other = lax.optimization_barrier((d_own, b_other))
    d_other = lax.ppermute(d_own, "c", swap)
    parts = exchange_rows(d_own, d_other, b_own, b_other)
    parts = lax.all_to_all(parts, ("x", "y"), 0, 0, tiled=True)
    parts = lax.all_to_all(sum_xy(parts), ("z", "c"), 0, 0, tiled=True)
    total_ri = three_center.shape[0] * Z * X * C * Y
    return sum_z(parts, 1.0 / math.sqrt(total_ri * A)).T


def solution(mesh):
    fine = Mesh(mesh.devices.reshape(Z, X, C, Y), ("z", "x", "c", "y"))
    every = ("z", "x", "c", "y")
    return jax.shard_map(
        per_device,
        mesh=fine,
        in_specs=(P(every, None, None), P(every, None, None), P("y", None), P()),
        out_specs=P("y", ("z", "x", "c")),
        check_vma=False,
    )
```

time: 84.8 us -> 84.8 us (level)
  starting transfers between devices: 22.3 us -> 21.4 us
  waiting for transfers between devices: 4.73 us -> 5.6 us
    ppermute x1, starting transfers between devices: 6.44 us -> 5.55 us  [per_device(): d_other = lax.ppermute(d_own, 'c', swap)]
    ppermute x1, waiting for transfers between devices: 2.84 us -> 3.71 us  [per_device(): b_other = lax.ppermute(b_own, 'c', swap)]
  transfers between devices with their start and end apart: 3 -> 3, of which waited for: 3 -> 3; matrix products, arithmetic and copies ran while one was open for 0% -> 0% of each run, Pallas kernels for 3% -> 2%
where the time goes in v5:
time: 84.8 us; the launch traced here: 84.1 us
  blocking collectives  45.8 us (54%)
  starting transfers between devices  21.4 us (25%)
  Pallas kernels  11.3 us (13%)
  waiting for transfers between devices  5.6 us (7%)
    all_to_all x1, blocking collectives, per_device(): parts = lax.all_to_all(sum_xy(parts), ('z', 'c'), 0, 0, tiled=True)  26.5 us
    all_to_all x1, blocking collectives, per_device(): parts = lax.all_to_all(parts, ('x', 'y'), 0, 0, tiled=True)  19.3 us
    ppermute x1, starting transfers between devices, per_device(): b_other = lax.ppermute(b_own, 'c', swap)  8.24 us
    all_to_all x1, starting transfers between devices, per_device(): d_own = settle(lax.all_to_all(mine, 'y', 0, 0, tiled=True))  7.65 us
    pallas_call x1, Pallas kernels, exchange_rows(): pl.pallas_call(functools.partial(exchange_kernel, count), in_specs=[VMEM,...  6.55 us
    ppermute x1, starting transfers between devices, per_device(): d_other = lax.ppermute(d_own, 'c', swap)  5.55 us
    ppermute x1, waiting for transfers between devices, per_device(): b_other = lax.ppermute(b_own, 'c', swap)  3.71 us
    pallas_call x1, Pallas kernels, mask_and_order(): pl.pallas_call(mask_kernel, grid=(count,), in_specs=[SMEM, spec], out_spe...  1.94 us
  transfers between devices with their start and end apart: 3, of which 3 were waited for; matrix products, arithmetic and copies ran while one was open for 0% of the time, Pallas kernels for 2%

profile of v5, /device:TPU:1, one launch (start us, length us, event | category | flops | bytes accessed | tf_op | source)
XLA Modules:
  0.0 84.1 jit_solution(14803909834018617837)
XLA Ops:
  0.0 1.8 %pack.1 = bf16[8,96,256]{2,1,0:T(8,128)(2,1)} custom-call(s32[6,6]{1,0:T(8,128)} %d_pattern.1, bf16[96,768]{1,0:T(8,128)(2,1)} %density.1), custom_call_target="tpu_custom_call" | custom-call | tf_op jit(solution)/shard_map/pack/pallas_call | solution.py:162
  1.8 7.7 %all-to-all-start = ((bf16[8,96,256]{2,1,0:T(8,128)(2,1)}), bf16[8,96,256]{2,1,0:T(8,128)(2,1)S(1)}, u32[]{:S(2)}, u32[]{:S(2)}) async-start(bf16[8,96,256]{2,1,0:T(8,128)(2,1)} %pack.1), calls=%async_computation | async-start | bytes 786432 | tf_op jit(solution)/shard_map/all_to_all | solution.py:225
  9.4 1.9 %mask.1.b_own = bf16[2,48,16,768]{3,2,1,0:T(8,128)(2,1)S(1)} custom-call(s32[6,2,6]{2,1,0:T(2,128)} %bitcast.4, bf16[2,48,16,768]{3,2,1,0:T(8,128)(2,1)} %bitcast.3), custom_call_target="tpu_custom_call" | custom-call | flops 99999997952 | tf_op jit(solution)/shard_map/mask/pallas_call | solution.py:55
  11.4 8.2 %collective-permute-start = (bf16[2,48,16,768]{3,2,1,0:T(8,128)(2,1)S(1)}, bf16[2,48,16,768]{3,2,1,0:T(8,128)(2,1)}, u32[]{:S(2)}, u32[]{:S(2)}) collective-permute-start(bf16[2,48,16,768]{3,2,1,0:T(8,128)(2,1)S(1)} %mask.1.b_own), channel_id=1, source_target_pairs={{0,8},{8,0},{1,9},{9,1},{2,10},{10,2},{3,11},{11,3},{4,12},{12,4},... | collective-permute-start | bytes 7077896 | tf_op jit(solution)/shard_map/ppermute | solution.py:224
  19.6 0.6 all-to-all-done.in_ref
  20.2 3.7 %collective-permute-done.b_there = bf16[2,48,16,768]{3,2,1,0:T(8,128)(2,1)} collective-permute-done((bf16[2,48,16,768]{3,2,1,0:T(8,128)(2,1)S(1)}, bf16[2,48,16,768]{3,2,1,0:T(8,128)(2,1)}, u32[]{:S(2)}, u32[]{:S(2)}) %collective-permute-start) | collective-permute-done | bytes 2359328 | tf_op jit(solution)/shard_map/ppermute | solution.py:224
  23.9 5.6 %collective-permute-start.1 = (bf16[8,96,256]{2,1,0:T(8,128)(2,1)S(1)}, bf16[8,96,256]{2,1,0:T(8,128)(2,1)S(1)}, u32[]{:S(2)}, u32[]{:S(2)}) collective-permute-start(bf16[8,96,256]{2,1,0:T(8,128)(2,1)S(1)} %settle.1.d_own), channel_id=1, source_target_pairs={{0,8},{8,0},{1,9},{9,1},{2,10},{10,2},{3,11},{11,3},{4,12},{12,4},... | collective-permute-start | bytes 1179656 | tf_op jit(solution)/shard_map/ppermute | solution.py:227
  29.4 1.3 %collective-permute-done.1.d_other = bf16[8,96,256]{2,1,0:T(8,128)(2,1)S(1)} collective-permute-done((bf16[8,96,256]{2,1,0:T(8,128)(2,1)S(1)}, bf16[8,96,256]{2,1,0:T(8,128)(2,1)S(1)}, u32[]{:S(2)}, u32[]{:S(2)}) %collective-permute-start.1) | collective-permute-done | bytes 393248 | tf_op jit(solution)/shard_map/ppermute | solution.py:227
  30.8 6.5 %exchange.1 = bf16[32,72,128]{2,1,0:T(8,128)(2,1)S(1)} custom-call(bf16[8,96,256]{2,1,0:T(8,128)(2,1)S(1)} %settle.1.d_own, bf16[8,96,256]{2,1,0:T(8,128)(2,1)S(1)} %collective-permute-done.1.d_other, bf16[2,48,16,768]{3,2,1,0:T(8,128)(2,1)S(1)} %mask.1.b_own, bf16[2,48,16,768]{3,2,1,0:T(8,128)(2,1)} %collective-permute-done.b_there), custom_call_target="tpu_custom_call" | custom-call | tf_op jit(solution)/shard_map/exchange/pallas_call | solution.py:132
  37.3 19.3 %all_to_all.15.in_ref = bf16[32,72,128]{2,1,0:T(8,128)(2,1)S(1)} all-to-all(bf16[32,72,128]{2,1,0:T(8,128)(2,1)S(1)} %exchange.1), channel_id=1, replica_groups=mesh['z'=12,'x'=4,'c'=2,'y'=8] {'x','y'}, dimensions={0} | all-to-all | bytes 1179648 | tf_op jit(solution)/shard_map/all_to_all | solution.py:229
  56.6 0.3 sum_xy.1
  56.9 26.5 %all_to_all.16.in_ref = f32[24,4,128]{2,1,0:T(4,128)S(1)} all-to-all(f32[24,4,128]{2,1,0:T(4,128)S(1)} %sum_xy.1), channel_id=1, replica_groups=mesh['z'=12,'x'=4,'c'=2,'y'=8] {'z','c'}, dimensions={0} | all-to-all | bytes 98304 | tf_op jit(solution)/shard_map/all_to_all | solution.py:230
  83.4 0.7 sum_z.1
  (1 shorter events, 0.0 us)
Async XLA Ops:
  1.8 18.4 %all-to-all-start = ((bf16[8,96,256]{2,1,0:T(8,128)(2,1)}), bf16[8,96,256]{2,1,0:T(8,128)(2,1)S(1)}, u32[]{:S(2)}, u32[]{:S(2)}) async-start(bf16[8,96,256]{2,1,0:T(8,128)(2,1)} %pack.1), calls=%async_computation | async-start | bytes 786432 | tf_op jit(solution)/shard_map/all_to_all | solution.py:225
  11.4 12.5 %collective-permute-start = (bf16[2,48,16,768]{3,2,1,0:T(8,128)(2,1)S(1)}, bf16[2,48,16,768]{3,2,1,0:T(8,128)(2,1)}, u32[]{:S(2)}, u32[]{:S(2)}) collective-permute-start(bf16[2,48,16,768]{3,2,1,0:T(8,128)(2,1)S(1)} %mask.1.b_own), channel_id=1, source_target_pairs={{0,8},{8,0},{1,9},{9,1},{2,10},{10,2},{3,11},{11,3},{4,12},{12,4},... | collective-permute-start | bytes 7077896 | tf_op jit(solution)/shard_map/ppermute | solution.py:224
  23.9 6.9 %collective-permute-start.1 = (bf16[8,96,256]{2,1,0:T(8,128)(2,1)S(1)}, bf16[8,96,256]{2,1,0:T(8,128)(2,1)S(1)}, u32[]{:S(2)}, u32[]{:S(2)}) collective-permute-start(bf16[8,96,256]{2,1,0:T(8,128)(2,1)S(1)} %settle.1.d_own), channel_id=1, source_target_pairs={{0,8},{8,0},{1,9},{9,1},{2,10},{10,2},{3,11},{11,3},{4,12},{12,4},... | collective-permute-start | bytes 1179656 | tf_op jit(solution)/shard_map/ppermute | solution.py:227

commit v6 on v5

--- a/solution.py
+++ b/solution.py
@@ -77,9 +77,30 @@
     )(part)
 
 
-def exchange_kernel(count, d_own, d_other, b_own, b_there, out_ref, d, acc, b_other, arrived):
-    fetch = pltpu.make_async_copy(b_there, b_other, arrived)
-    fetch.start()
+def bring_kernel(*refs):
+    arrived = refs[-1]
+    count = len(refs) // 2
+    copies = [pltpu.make_async_copy(refs[i], refs[count + i], arrived.at[i]) for i in range(count)]
+    for copy in copies:
+        copy.start()
+    for copy in copies:
+        copy.wait()
+
+
+def bring(*there):
+    return pl.pallas_call(
+        bring_kernel,
+        in_specs=[ANY] * len(there),
+        out_specs=[VMEM] * len(there),
+        out_shape=[pltpu.VMEM(x.shape, x.dtype) for x in there],
+        scratch_shapes=[pltpu.SemaphoreType.DMA((len(there),))],
+        cost_estimate=pl.CostEstimate(flops=0, bytes_accessed=sum(x.size * 4 for x in there), transcendentals=0),
+        compiler_params=pltpu.CompilerParams(vmem_limit_bytes=MIB),
+        name="bring",
+    )(*there)
+
+
+def exchange_kernel(count, d_own, d_other, b_own, b_other, out_ref, d, acc):
     core = lax.axis_index("c")
     for h, part in ((core, d_own), (1 - core, d_other)):
         for y in range(Y):
@@ -99,50 +120,43 @@
     top, bottom = slice(0, ROWS // 2), slice(ROWS // 2, ROWS)
     half_rows, halves = Z * G, X // 2
     for p in range(2 * count):
-        if p == count:
-            fetch.wait()
         b = b_own.at[p] if p < count else b_other.at[p - count]
+        full = b[...].reshape(A, A)
         rows = [b[pl.ds((2 * q + core) * Z, Z)].reshape(half_rows, A) for q in range(halves)]
         half = jnp.dot(jnp.concatenate(rows, 0), d[...], preferred_element_type=jnp.float32).astype(jnp.bfloat16)
+        term = lax.dot_general(half, full, (((1,), (1,)), ((), ())), preferred_element_type=jnp.float32)
+        acc[...] = term if p == 0 else acc[...] + term
+    for y in range(Y):
+        at = []
+        for t in range(ROWS // G):
+            z, x = divmod(y * (YROWS // G) + 2 * t, X)
+            at.append((x // 2) * half_rows + z * G)
         for q in range(halves):
-            full = b[q * 2 * Z : (q + 1) * 2 * Z].reshape(2 * half_rows, A)
-            term = lax.dot_general(half, full, (((1,), (1,)), ((), ())), preferred_element_type=jnp.float32)
-            cols = slice(q * 2 * half_rows, (q + 1) * 2 * half_rows)
-            total = term if p == 0 else acc[:, cols] + term
-            if p < 2 * count - 1:
-                acc[:, cols] = total
-                continue
-            for y in range(Y):
-                groups = []
-                for t in range(ROWS // G):
-                    z, x = divmod(y * (YROWS // G) + 2 * t, X)
-                    at = (x // 2) * half_rows + z * G
-                    groups.append(total[at : at + G])
-                block = jnp.concatenate(groups, 0)
-                first, middle, last = block[:, :128], block[:, 128:256], block[:, 256:]
-                turned = pltpu.roll(middle, 64, 1)
-                even = jnp.where(lane < 64, middle[top], turned[bottom])
-                odd = jnp.where(lane < 64, turned[top], middle[bottom])
-                out_ref[(2 * q) * Y + y] = jnp.concatenate([first, even], 0).astype(jnp.bfloat16)
-                out_ref[(2 * q + 1) * Y + y] = jnp.concatenate([last, odd], 0).astype(jnp.bfloat16)
+            left, middle, right = [
+                jnp.concatenate([acc[r : r + G, (3 * q + i) * 128 : (3 * q + i + 1) * 128] for r in at], 0)
+                for i in range(3)
+            ]
+            turned = pltpu.roll(middle, 64, 1)
+            even = jnp.where(lane < 64, middle[top], turned[bottom])
+            odd = jnp.where(lane < 64, turned[top], middle[bottom])
+            out_ref[(2 * q) * Y + y] = jnp.concatenate([left, even], 0).astype(jnp.bfloat16)
+            out_ref[(2 * q + 1) * Y + y] = jnp.concatenate([right, odd], 0).astype(jnp.bfloat16)
 
 
 def exchange_rows(d_own, d_other, b_own, b_other):
     count = b_own.shape[0]
     return pl.pallas_call(
         functools.partial(exchange_kernel, count),
-        in_specs=[VMEM, VMEM, VMEM, ANY],
+        in_specs=[VMEM, VMEM, VMEM, VMEM],
         out_specs=VMEM,
         out_shape=pltpu.VMEM((X * Y, PACK, 128), jnp.bfloat16),
         scratch_shapes=[
             pltpu.VMEM((A, A), jnp.bfloat16),
             pltpu.VMEM((Y * ROWS, A), jnp.float32),
-            pltpu.VMEM(b_other.shape, jnp.bfloat16),
-            pltpu.SemaphoreType.DMA,
         ],
         compiler_params=pltpu.CompilerParams(vmem_limit_bytes=24 * MIB),
         name="exchange",
-    )(vmem(d_own), vmem(d_other), vmem(b_own), b_other)
+    )(vmem(d_own), vmem(d_other), vmem(b_own), vmem(b_other))
 
 
 def pack_kernel(d_pattern, density, out_ref):
@@ -223,9 +237,9 @@
     b_own = mask_and_order(three_center, b_pattern)
     b_other = lax.ppermute(b_own, "c", swap)
     d_own = settle(lax.all_to_all(mine, "y", 0, 0, tiled=True))
-    d_own, b_other = lax.optimization_barrier((d_own, b_other))
+    d_own, b_own, b_other = lax.optimization_barrier((d_own, b_own, b_other))
     d_other = lax.ppermute(d_own, "c", swap)
-    parts = exchange_rows(d_own, d_other, b_own, b_other)
+    parts = exchange_rows(d_own, d_other, *bring(b_own, b_other))
     parts = lax.all_to_all(parts, ("x", "y"), 0, 0, tiled=True)
     parts = lax.all_to_all(sum_xy(parts), ("z", "c"), 0, 0, tiled=True)
     total_ri = three_center.shape[0] * Z * X * C * Y

time: 84.8 us -> 83 us (0.979)
  waiting for transfers between devices: 5.6 us -> 4.27 us
    pallas_call x1, Pallas kernels: 6.55 us -> 4.23 us  [exchange_rows(): pl.pallas_call(functools.partial(exchange_kernel, count), in_specs=[VMEM,...]
    pallas_call x0 -> x1, Pallas kernels: none -> 1.84 us  [bring(): pl.pallas_call(bring_kernel, in_specs=[ANY] * len(there), out_specs=[VMEM...]
    ppermute x1, waiting for transfers between devices: 1.33 us -> 0.01 us  [per_device(): d_other = lax.ppermute(d_own, 'c', swap)]
  transfers between devices with their start and end apart: 3 -> 3, of which waited for: 3 -> 2; matrix products, arithmetic and copies ran while one was open for 0% -> 0% of each run, Pallas kernels for 2% -> 5%
where the time goes in v6:
time: 83 us; the launch traced here: 82.4 us
  blocking collectives  45.8 us (55%)
  starting transfers between devices  21.4 us (26%)
  Pallas kernels  10.8 us (13%)
  waiting for transfers between devices  4.27 us (5%)
    all_to_all x1, blocking collectives, per_device(): parts = lax.all_to_all(sum_xy(parts), ('z', 'c'), 0, 0, tiled=True)  26.3 us
    all_to_all x1, blocking collectives, per_device(): parts = lax.all_to_all(parts, ('x', 'y'), 0, 0, tiled=True)  19.5 us
    ppermute x1, starting transfers between devices, per_device(): b_other = lax.ppermute(b_own, 'c', swap)  8.24 us
    all_to_all x1, starting transfers between devices, per_device(): d_own = settle(lax.all_to_all(mine, 'y', 0, 0, tiled=True))  7.65 us
    ppermute x1, starting transfers between devices, per_device(): d_other = lax.ppermute(d_own, 'c', swap)  5.55 us
    pallas_call x1, Pallas kernels, exchange_rows(): pl.pallas_call(functools.partial(exchange_kernel, count), in_specs=[VMEM,...  4.23 us
    ppermute x1, waiting for transfers between devices, per_device(): b_other = lax.ppermute(b_own, 'c', swap)  3.71 us
    pallas_call x1, Pallas kernels, mask_and_order(): pl.pallas_call(mask_kernel, grid=(count,), in_specs=[SMEM, spec], out_spe...  1.94 us
  transfers between devices with their start and end apart: 3, of which 2 were waited for; matrix products, arithmetic and copies ran while one was open for 0% of the time, Pallas kernels for 5%

profile of v6, /device:TPU:1, one launch (start us, length us, event | category | flops | bytes accessed | tf_op | source)
XLA Modules:
  0.0 82.4 jit_solution(11347141155100822927)
XLA Ops:
  0.0 1.8 %pack.1 = bf16[8,96,256]{2,1,0:T(8,128)(2,1)} custom-call(s32[6,6]{1,0:T(8,128)} %d_pattern.1, bf16[96,768]{1,0:T(8,128)(2,1)} %density.1), custom_call_target="tpu_custom_call" | custom-call | tf_op jit(solution)/shard_map/pack/pallas_call | solution.py:176
  1.8 7.7 %all-to-all-start = ((bf16[8,96,256]{2,1,0:T(8,128)(2,1)}), bf16[8,96,256]{2,1,0:T(8,128)(2,1)S(1)}, u32[]{:S(2)}, u32[]{:S(2)}) async-start(bf16[8,96,256]{2,1,0:T(8,128)(2,1)} %pack.1), calls=%async_computation | async-start | bytes 786432 | tf_op jit(solution)/shard_map/all_to_all | solution.py:239
  9.4 1.9 %mask.1.refs_0_ = bf16[2,48,16,768]{3,2,1,0:T(8,128)(2,1)S(1)} custom-call(s32[6,2,6]{2,1,0:T(2,128)} %bitcast.4, bf16[2,48,16,768]{3,2,1,0:T(8,128)(2,1)} %bitcast.3), custom_call_target="tpu_custom_call" | custom-call | flops 99999997952 | tf_op jit(solution)/shard_map/mask/pallas_call | solution.py:55
  11.4 8.2 %collective-permute-start = (bf16[2,48,16,768]{3,2,1,0:T(8,128)(2,1)S(1)}, bf16[2,48,16,768]{3,2,1,0:T(8,128)(2,1)}, u32[]{:S(2)}, u32[]{:S(2)}) collective-permute-start(bf16[2,48,16,768]{3,2,1,0:T(8,128)(2,1)S(1)} %mask.1.refs_0_), channel_id=1, source_target_pairs={{0,8},{8,0},{1,9},{9,1},{2,10},{10,2},{3,11},{11,3},{4,12},{12,4},... | collective-permute-start | bytes 7077896 | tf_op jit(solution)/shard_map/ppermute | solution.py:238
  19.6 0.6 all-to-all-done.in_ref
  20.2 3.7 %collective-permute-done.refs_1_ = bf16[2,48,16,768]{3,2,1,0:T(8,128)(2,1)} collective-permute-done((bf16[2,48,16,768]{3,2,1,0:T(8,128)(2,1)S(1)}, bf16[2,48,16,768]{3,2,1,0:T(8,128)(2,1)}, u32[]{:S(2)}, u32[]{:S(2)}) %collective-permute-start) | collective-permute-done | bytes 2359328 | tf_op jit(solution)/shard_map/ppermute | solution.py:238
  23.9 5.6 %collective-permute-start.1 = (bf16[8,96,256]{2,1,0:T(8,128)(2,1)S(1)}, bf16[8,96,256]{2,1,0:T(8,128)(2,1)S(1)}, u32[]{:S(2)}, u32[]{:S(2)}) collective-permute-start(bf16[8,96,256]{2,1,0:T(8,128)(2,1)S(1)} %settle.1.d_own), channel_id=1, source_target_pairs={{0,8},{8,0},{1,9},{9,1},{2,10},{10,2},{3,11},{11,3},{4,12},{12,4},... | collective-permute-start | bytes 1179656 | tf_op jit(solution)/shard_map/ppermute | solution.py:241
  29.4 1.8 %bring.1 = (bf16[2,48,16,768]{3,2,1,0:T(8,128)(2,1)S(1)}, bf16[2,48,16,768]{3,2,1,0:T(8,128)(2,1)S(1)}) custom-call(bf16[2,48,16,768]{3,2,1,0:T(8,128)(2,1)S(1)} %mask.1.refs_0_, bf16[2,48,16,768]{3,2,1,0:T(8,128)(2,1)} %collective-permute-done.refs_1_), custom_call_target="tpu_custom_call" | custom-call | bytes 9437184 | tf_op jit(solution)/shard_map/bring/pallas_call | solution.py:91
  31.3 0.0 collective-permute-done.1.d_other
  31.3 4.2 %exchange.1 = bf16[32,72,128]{2,1,0:T(8,128)(2,1)S(1)} custom-call(bf16[8,96,256]{2,1,0:T(8,128)(2,1)S(1)} %settle.1.d_own, bf16[8,96,256]{2,1,0:T(8,128)(2,1)S(1)} %collective-permute-done.1.d_other, bf16[2,48,16,768]{3,2,1,0:T(8,128)(2,1)S(1)} %get-tuple-element.17.b_own, bf16[2,48,16,768]{3,2,1,0:T(8,128)(2,1)S(1)} %get-tuple-element.18.b_other), custom_call_target="tpu_custom_call" | custom-call | tf_op jit(solution)/shard_map/exchange/pallas_call | solution.py:148
  35.5 19.5 %all_to_all.15.in_ref = bf16[32,72,128]{2,1,0:T(8,128)(2,1)S(1)} all-to-all(bf16[32,72,128]{2,1,0:T(8,128)(2,1)S(1)} %exchange.1), channel_id=1, replica_groups=mesh['z'=12,'x'=4,'c'=2,'y'=8] {'x','y'}, dimensions={0} | all-to-all | bytes 1179648 | tf_op jit(solution)/shard_map/all_to_all | solution.py:243
  55.1 0.3 sum_xy.1
  55.4 26.3 %all_to_all.16.in_ref = f32[24,4,128]{2,1,0:T(4,128)S(1)} all-to-all(f32[24,4,128]{2,1,0:T(4,128)S(1)} %sum_xy.1), channel_id=1, replica_groups=mesh['z'=12,'x'=4,'c'=2,'y'=8] {'z','c'}, dimensions={0} | all-to-all | bytes 98304 | tf_op jit(solution)/shard_map/all_to_all | solution.py:244
  81.6 0.7 sum_z.1
  (1 shorter events, 0.0 us)
Async XLA Ops:
  1.8 18.4 %all-to-all-start = ((bf16[8,96,256]{2,1,0:T(8,128)(2,1)}), bf16[8,96,256]{2,1,0:T(8,128)(2,1)S(1)}, u32[]{:S(2)}, u32[]{:S(2)}) async-start(bf16[8,96,256]{2,1,0:T(8,128)(2,1)} %pack.1), calls=%async_computation | async-start | bytes 786432 | tf_op jit(solution)/shard_map/all_to_all | solution.py:239
  11.4 12.5 %collective-permute-start = (bf16[2,48,16,768]{3,2,1,0:T(8,128)(2,1)S(1)}, bf16[2,48,16,768]{3,2,1,0:T(8,128)(2,1)}, u32[]{:S(2)}, u32[]{:S(2)}) collective-permute-start(bf16[2,48,16,768]{3,2,1,0:T(8,128)(2,1)S(1)} %mask.1.refs_0_), channel_id=1, source_target_pairs={{0,8},{8,0},{1,9},{9,1},{2,10},{10,2},{3,11},{11,3},{4,12},{12,4},... | collective-permute-start | bytes 7077896 | tf_op jit(solution)/shard_map/ppermute | solution.py:238
  23.9 7.4 %collective-permute-start.1 = (bf16[8,96,256]{2,1,0:T(8,128)(2,1)S(1)}, bf16[8,96,256]{2,1,0:T(8,128)(2,1)S(1)}, u32[]{:S(2)}, u32[]{:S(2)}) collective-permute-start(bf16[8,96,256]{2,1,0:T(8,128)(2,1)S(1)} %settle.1.d_own), channel_id=1, source_target_pairs={{0,8},{8,0},{1,9},{9,1},{2,10},{10,2},{3,11},{11,3},{4,12},{12,4},... | collective-permute-start | bytes 1179656 | tf_op jit(solution)/shard_map/ppermute | solution.py:241

commit v7 on v6

--- a/solution.py
+++ b/solution.py
@@ -9,6 +9,7 @@
 from jax.sharding import Mesh, PartitionSpec as P
 
 Z, X, C, Y = 12, 4, 2, 8
+ZP, YP = Z // 2, Y // 2
 A, BS, NB = 768, 128, 6
 K = 8
 G = 16
@@ -17,8 +18,9 @@
 YROWS = A // Y
 STEP = 32
 SENT = 4
-PACK = ROWS * Z * G // 128
-MAIN = 128 // G
+UNIT = 2 * G
+UNITS = 128 // UNIT
+TILES = ZP // 2
 COST = 10**11
 MIB = 1024 * 1024
 VMEM = pl.BlockSpec(memory_space=pltpu.VMEM)
@@ -35,7 +37,8 @@
 
 
 def place(z, x):
-    return x * Z + z
+    pair, lower = divmod(z, 2)
+    return ((x // 2 * TILES + pair // 2) * UNITS + x % 2 * 2 + lower) * 2 + pair % 2
 
 
 def mask_kernel(pattern, b_ref, out_ref):
@@ -116,31 +119,34 @@
             cb = (rb + k) % NB
             rows, cols = slice(rb * BS, (rb + 1) * BS), slice(cb * BS, (cb + 1) * BS)
             d[rows, cols] = d[cols, rows].T
-    lane = lax.broadcasted_iota(jnp.int32, (ROWS // 2, 128), 1)
-    top, bottom = slice(0, ROWS // 2), slice(ROWS // 2, ROWS)
-    half_rows, halves = Z * G, X // 2
+    unit = lax.broadcasted_iota(jnp.int32, (ROWS, 128), 1) // UNIT
+    runs = [pl.ds(i * 2 * UNITS + core * UNITS, UNITS) for i in range(X // 2 * TILES)]
     for p in range(2 * count):
         b = b_own.at[p] if p < count else b_other.at[p - count]
         full = b[...].reshape(A, A)
-        rows = [b[pl.ds((2 * q + core) * Z, Z)].reshape(half_rows, A) for q in range(halves)]
-        half = jnp.dot(jnp.concatenate(rows, 0), d[...], preferred_element_type=jnp.float32).astype(jnp.bfloat16)
+        rows = jnp.concatenate([b[run].reshape(UNITS * G, A) for run in runs], 0)
+        half = jnp.dot(rows, d[...], preferred_element_type=jnp.float32).astype(jnp.bfloat16)
         term = lax.dot_general(half, full, (((1,), (1,)), ((), ())), preferred_element_type=jnp.float32)
         acc[...] = term if p == 0 else acc[...] + term
-    for y in range(Y):
+    for yl in range(2):
         at = []
-        for t in range(ROWS // G):
-            z, x = divmod(y * (YROWS // G) + 2 * t, X)
-            at.append((x // 2) * half_rows + z * G)
-        for q in range(halves):
-            left, middle, right = [
-                jnp.concatenate([acc[r : r + G, (3 * q + i) * 128 : (3 * q + i + 1) * 128] for r in at], 0)
-                for i in range(3)
-            ]
-            turned = pltpu.roll(middle, 64, 1)
-            even = jnp.where(lane < 64, middle[top], turned[bottom])
-            odd = jnp.where(lane < 64, turned[top], middle[bottom])
-            out_ref[(2 * q) * Y + y] = jnp.concatenate([left, even], 0).astype(jnp.bfloat16)
-            out_ref[(2 * q + 1) * Y + y] = jnp.concatenate([right, odd], 0).astype(jnp.bfloat16)
+        for yp in range(YP):
+            for t in range(ROWS // G):
+                z, x = divmod((2 * yp + yl) * (YROWS // G) + 2 * t, X)
+                run, group = divmod(place(z, x), 2 * UNITS)
+                at.append((run * UNITS + group) * G)
+        for i in range(X // 2 * TILES):
+            lanes = slice(i * 128, (i + 1) * 128)
+            tiles = [acc[r : r + G, lanes] for r in at]
+            tiles = [jnp.concatenate(tiles[yp * (ROWS // G) : (yp + 1) * (ROWS // G)], 0) for yp in range(YP)]
+            for j in range(UNITS):
+                out = tiles[j]
+                for yp in range(YP):
+                    if yp != j:
+                        out = jnp.where(unit == yp, pltpu.roll(tiles[yp], (yp - j) % UNITS * UNIT, 1), out)
+                x, zl = i // TILES * 2 + j // 2, j % 2
+                here = slice(i % TILES * ROWS, (i % TILES + 1) * ROWS)
+                out_ref[(x * 2 + yl) * 2 + zl, here] = out.astype(jnp.bfloat16)
 
 
 def exchange_rows(d_own, d_other, b_own, b_other):
@@ -149,7 +155,7 @@
         functools.partial(exchange_kernel, count),
         in_specs=[VMEM, VMEM, VMEM, VMEM],
         out_specs=VMEM,
-        out_shape=pltpu.VMEM((X * Y, PACK, 128), jnp.bfloat16),
+        out_shape=pltpu.VMEM((X * 4, TILES * ROWS, 128), jnp.bfloat16),
         scratch_shapes=[
             pltpu.VMEM((A, A), jnp.bfloat16),
             pltpu.VMEM((Y * ROWS, A), jnp.float32),
@@ -160,7 +166,7 @@
 
 
 def pack_kernel(d_pattern, density, out_ref):
-    y, core = lax.axis_index("y"), lax.axis_index("c")
+    y, core = lax.axis_index("yp") * 2 + lax.axis_index("yl"), lax.axis_index("c")
     for t in range(YROWS // STEP):
         rb = lax.div(y * YROWS + t * STEP, BS)
         for j in range(SENT // C):
@@ -183,50 +189,47 @@
     )(hbm(d_pattern), hbm(density))
 
 
-def sum_xy_kernel(in_ref, out_ref):
+def sum_near_kernel(in_ref, out_ref):
     total = in_ref[0].astype(jnp.float32)
-    for i in range(1, X * Y):
+    for i in range(1, X * 4):
         total = total + in_ref[i].astype(jnp.float32)
-    first, rest = total[:ROWS].T, total[ROWS:].T
-    rest = jnp.concatenate([rest[:64], rest[64:]], 1)
-    odd = lax.rem(lax.axis_index("x"), 2)
-    for part, at in ((first, odd * (Z - MAIN) * C), (rest, (1 - odd) * MAIN * C)):
-        count = part.shape[0] // K
-        part = part.reshape(count, K, ROWS)
-        pad = jnp.zeros((count, K // 2, 128 - 2 * ROWS), jnp.float32)
-        out_ref[pl.ds(at, count)] = jnp.concatenate([part[:, : K // 2], part[:, K // 2 :], pad], 2)
-
-
-def sum_xy(parts):
-    return pl.pallas_call(
-        sum_xy_kernel,
+    for i in range(TILES):
+        part = total[i * ROWS : (i + 1) * ROWS].T
+        part = part.reshape(YP, 2 * C, K, ROWS)
+        pad = jnp.zeros((YP, 2 * C, K // 2, 128 - 2 * ROWS), jnp.float32)
+        out_ref[:, i * 2 * C : (i + 1) * 2 * C] = jnp.concatenate([part[:, :, : K // 2], part[:, :, K // 2 :], pad], 3)
+
+
+def sum_near(parts):
+    return pl.pallas_call(
+        sum_near_kernel,
         in_specs=[VMEM],
         out_specs=VMEM,
-        out_shape=pltpu.VMEM((Z * C, K // 2, 128), jnp.float32),
+        out_shape=pltpu.VMEM((YP, ZP * C, K // 2, 128), jnp.float32),
         compiler_params=pltpu.CompilerParams(vmem_limit_bytes=8 * MIB),
-        name="sum_xy",
+        name="sum_near",
     )(vmem(parts))
 
 
-def sum_z_kernel(factor, in_ref, out_ref):
+def sum_far_kernel(factor, in_ref, out_ref):
     halves = []
     for c in range(C):
         total = in_ref[c]
-        for z in range(1, Z):
-            total = total + in_ref[z * C + c]
+        for i in range(1, YP * ZP):
+            total = total + in_ref[i * C + c]
         total = jnp.concatenate([total[:, :ROWS], total[:, ROWS : 2 * ROWS]], 0)
         halves.append(total * factor)
     out_ref[...] = jnp.concatenate([halves[g % C][:, g // C * G : (g // C + 1) * G] for g in range(YROWS // G)], 1)
 
 
-def sum_z(parts, factor):
-    return pl.pallas_call(
-        functools.partial(sum_z_kernel, factor),
+def sum_far(parts, factor):
+    return pl.pallas_call(
+        functools.partial(sum_far_kernel, factor),
         in_specs=[VMEM],
         out_specs=VMEM,
         out_shape=jax.ShapeDtypeStruct((K, YROWS), jnp.float32),
         compiler_params=pltpu.CompilerParams(vmem_limit_bytes=4 * MIB),
-        name="sum_z",
+        name="sum_far",
     )(vmem(parts))
 
 
@@ -236,23 +239,24 @@
     mine, b_pattern = lax.optimization_barrier((mine, b_pattern))
     b_own = mask_and_order(three_center, b_pattern)
     b_other = lax.ppermute(b_own, "c", swap)
-    d_own = settle(lax.all_to_all(mine, "y", 0, 0, tiled=True))
+    d_own = settle(lax.all_to_all(mine, ("yp", "yl"), 0, 0, tiled=True))
     d_own, b_own, b_other = lax.optimization_barrier((d_own, b_own, b_other))
     d_other = lax.ppermute(d_own, "c", swap)
     parts = exchange_rows(d_own, d_other, *bring(b_own, b_other))
-    parts = lax.all_to_all(parts, ("x", "y"), 0, 0, tiled=True)
-    parts = lax.all_to_all(sum_xy(parts), ("z", "c"), 0, 0, tiled=True)
+    parts = lax.all_to_all(parts, ("x", "yl", "zl"), 0, 0, tiled=True)
+    parts = sum_near(parts).reshape(YP * ZP * C, K // 2, 128)
+    parts = lax.all_to_all(parts, ("yp", "zp", "c"), 0, 0, tiled=True)
     total_ri = three_center.shape[0] * Z * X * C * Y
-    return sum_z(parts, 1.0 / math.sqrt(total_ri * A)).T
+    return sum_far(parts, 1.0 / math.sqrt(total_ri * A)).T
 
 
 def solution(mesh):
-    fine = Mesh(mesh.devices.reshape(Z, X, C, Y), ("z", "x", "c", "y"))
-    every = ("z", "x", "c", "y")
+    every = ("zp", "zl", "x", "c", "yp", "yl")
+    fine = Mesh(mesh.devices.reshape(ZP, 2, X, C, YP, 2), every)
     return jax.shard_map(
         per_device,
         mesh=fine,
-        in_specs=(P(every, None, None), P(every, None, None), P("y", None), P()),
-        out_specs=P("y", ("z", "x", "c")),
+        in_specs=(P(every, None, None), P(every, None, None), P(("yp", "yl"), None), P()),
+        out_specs=P(("yp", "yl"), ("zp", "zl", "x", "c")),
         check_vma=False,
     )

time: 83 us -> 83.5 us (level)
  no operation moved by 1% of the time
where the time goes in v7:
time: 83.5 us; the launch traced here: 83.1 us
  blocking collectives  46.5 us (56%)
  starting transfers between devices  21.4 us (26%)
  Pallas kernels  10.9 us (13%)
  waiting for transfers between devices  4.27 us (5%)
    all_to_all x1, blocking collectives, per_device(): parts = lax.all_to_all(parts, ('yp', 'zp', 'c'), 0, 0, tiled=True)  32.2 us
    all_to_all x1, blocking collectives, per_device(): parts = lax.all_to_all(parts, ('x', 'yl', 'zl'), 0, 0, tiled=True)  14.3 us
    ppermute x1, starting transfers between devices, per_device(): b_other = lax.ppermute(b_own, 'c', swap)  8.24 us
    all_to_all x1, starting transfers between devices, per_device(): d_own = settle(lax.all_to_all(mine, ('yp', 'yl'), 0, 0, tiled=True))  7.65 us
    ppermute x1, starting transfers between devices, per_device(): d_other = lax.ppermute(d_own, 'c', swap)  5.55 us
    pallas_call x1, Pallas kernels, exchange_rows(): pl.pallas_call(functools.partial(exchange_kernel, count), in_specs=[VMEM,...  4.33 us
    ppermute x1, waiting for transfers between devices, per_device(): b_other = lax.ppermute(b_own, 'c', swap)  3.71 us
    pallas_call x1, Pallas kernels, mask_and_order(): pl.pallas_call(mask_kernel, grid=(count,), in_specs=[SMEM, spec], out_spe...  1.94 us
  transfers between devices with their start and end apart: 3, of which 2 were waited for; matrix products, arithmetic and copies ran while one was open for 0% of the time, Pallas kernels for 5%

profile of v7, /device:TPU:1, one launch (start us, length us, event | category | flops | bytes accessed | tf_op | source)
XLA Modules:
  0.0 83.1 jit_solution(2877463875304226422)
XLA Ops:
  0.0 1.8 %pack.1 = bf16[8,96,256]{2,1,0:T(8,128)(2,1)} custom-call(s32[6,6]{1,0:T(8,128)} %d_pattern.1, bf16[96,768]{1,0:T(8,128)(2,1)} %density.1), custom_call_target="tpu_custom_call" | custom-call | tf_op jit(solution)/shard_map/pack/pallas_call | solution.py:182
  1.8 7.7 %all-to-all-start = ((bf16[8,96,256]{2,1,0:T(8,128)(2,1)}), bf16[8,96,256]{2,1,0:T(8,128)(2,1)S(1)}, u32[]{:S(2)}, u32[]{:S(2)}) async-start(bf16[8,96,256]{2,1,0:T(8,128)(2,1)} %pack.1), calls=%async_computation | async-start | bytes 786432 | tf_op jit(solution)/shard_map/all_to_all | solution.py:242
  9.4 1.9 %mask.1.refs_0_ = bf16[2,48,16,768]{3,2,1,0:T(8,128)(2,1)S(1)} custom-call(s32[6,2,6]{2,1,0:T(2,128)} %bitcast.6, bf16[2,48,16,768]{3,2,1,0:T(8,128)(2,1)} %bitcast.5), custom_call_target="tpu_custom_call" | custom-call | flops 99999997952 | tf_op jit(solution)/shard_map/mask/pallas_call | solution.py:58
  11.4 8.2 %collective-permute-start = (bf16[2,48,16,768]{3,2,1,0:T(8,128)(2,1)S(1)}, bf16[2,48,16,768]{3,2,1,0:T(8,128)(2,1)}, u32[]{:S(2)}, u32[]{:S(2)}) collective-permute-start(bf16[2,48,16,768]{3,2,1,0:T(8,128)(2,1)S(1)} %mask.1.refs_0_), channel_id=1, source_target_pairs={{0,8},{8,0},{1,9},{9,1},{2,10},{10,2},{3,11},{11,3},{4,12},{12,4},... | collective-permute-start | bytes 7077896 | tf_op jit(solution)/shard_map/ppermute | solution.py:241
  19.6 0.6 all-to-all-done.in_ref
  20.2 3.7 %collective-permute-done.refs_1_ = bf16[2,48,16,768]{3,2,1,0:T(8,128)(2,1)} collective-permute-done((bf16[2,48,16,768]{3,2,1,0:T(8,128)(2,1)S(1)}, bf16[2,48,16,768]{3,2,1,0:T(8,128)(2,1)}, u32[]{:S(2)}, u32[]{:S(2)}) %collective-permute-start) | collective-permute-done | bytes 2359328 | tf_op jit(solution)/shard_map/ppermute | solution.py:241
  23.9 5.6 %collective-permute-start.1 = (bf16[8,96,256]{2,1,0:T(8,128)(2,1)S(1)}, bf16[8,96,256]{2,1,0:T(8,128)(2,1)S(1)}, u32[]{:S(2)}, u32[]{:S(2)}) collective-permute-start(bf16[8,96,256]{2,1,0:T(8,128)(2,1)S(1)} %settle.1.d_own), channel_id=1, source_target_pairs={{0,8},{8,0},{1,9},{9,1},{2,10},{10,2},{3,11},{11,3},{4,12},{12,4},... | collective-permute-start | bytes 1179656 | tf_op jit(solution)/shard_map/ppermute | solution.py:244
  29.4 1.8 %bring.1 = (bf16[2,48,16,768]{3,2,1,0:T(8,128)(2,1)S(1)}, bf16[2,48,16,768]{3,2,1,0:T(8,128)(2,1)S(1)}) custom-call(bf16[2,48,16,768]{3,2,1,0:T(8,128)(2,1)S(1)} %mask.1.refs_0_, bf16[2,48,16,768]{3,2,1,0:T(8,128)(2,1)} %collective-permute-done.refs_1_), custom_call_target="tpu_custom_call" | custom-call | bytes 9437184 | tf_op jit(solution)/shard_map/bring/pallas_call | solution.py:94
  31.3 0.0 collective-permute-done.1.d_other
  31.3 4.3 %exchange.1 = bf16[16,144,128]{2,1,0:T(8,128)(2,1)S(1)} custom-call(bf16[8,96,256]{2,1,0:T(8,128)(2,1)S(1)} %settle.1.d_own, bf16[8,96,256]{2,1,0:T(8,128)(2,1)S(1)} %collective-permute-done.1.d_other, bf16[2,48,16,768]{3,2,1,0:T(8,128)(2,1)S(1)} %get-tuple-element.17.b_own, bf16[2,48,16,768]{3,2,1,0:T(8,128)(2,1)S(1)} %get-tuple-element.18.b_other), custom_call_target="tpu_custom_call" | custom-call | tf_op jit(solution)/shard_map/exchange/pallas_call | solution.py:154
  35.6 14.3 %all_to_all.15.in_ref = bf16[16,144,128]{2,1,0:T(8,128)(2,1)S(1)} all-to-all(bf16[16,144,128]{2,1,0:T(8,128)(2,1)S(1)} %exchange.1), channel_id=1, replica_groups=mesh['zp'=6,'zl'=2,'x'=4,'c'=2,'yp'=4,'yl'=2] {'x','yl','zl'}, dimensions={0} | all-to-all | bytes 1179648 | tf_op jit(solution)/shard_map/all_to_all | solution.py:246
  49.9 0.2 sum_near.1
  50.2 32.2 %all_to_all.16.in_ref = f32[48,4,128]{2,1,0:T(4,128)S(1)} all-to-all(f32[48,4,128]{2,1,0:T(4,128)S(1)} %bitcast.4), channel_id=1, replica_groups=mesh['zp'=6,'zl'=2,'x'=4,'c'=2,'yp'=4,'yl'=2] {'yp','zp','c'}, dimensions={0} | all-to-all | bytes 196608 | tf_op jit(solution)/shard_map/all_to_all | solution.py:248
  82.4 0.8 sum_far.1
  (1 shorter events, 0.0 us)
Async XLA Ops:
  1.8 18.4 %all-to-all-start = ((bf16[8,96,256]{2,1,0:T(8,128)(2,1)}), bf16[8,96,256]{2,1,0:T(8,128)(2,1)S(1)}, u32[]{:S(2)}, u32[]{:S(2)}) async-start(bf16[8,96,256]{2,1,0:T(8,128)(2,1)} %pack.1), calls=%async_computation | async-start | bytes 786432 | tf_op jit(solution)/shard_map/all_to_all | solution.py:242
  11.4 12.5 %collective-permute-start = (bf16[2,48,16,768]{3,2,1,0:T(8,128)(2,1)S(1)}, bf16[2,48,16,768]{3,2,1,0:T(8,128)(2,1)}, u32[]{:S(2)}, u32[]{:S(2)}) collective-permute-start(bf16[2,48,16,768]{3,2,1,0:T(8,128)(2,1)S(1)} %mask.1.refs_0_), channel_id=1, source_target_pairs={{0,8},{8,0},{1,9},{9,1},{2,10},{10,2},{3,11},{11,3},{4,12},{12,4},... | collective-permute-start | bytes 7077896 | tf_op jit(solution)/shard_map/ppermute | solution.py:241
  23.9 7.4 %collective-permute-start.1 = (bf16[8,96,256]{2,1,0:T(8,128)(2,1)S(1)}, bf16[8,96,256]{2,1,0:T(8,128)(2,1)S(1)}, u32[]{:S(2)}, u32[]{:S(2)}) collective-permute-start(bf16[8,96,256]{2,1,0:T(8,128)(2,1)S(1)} %settle.1.d_own), channel_id=1, source_target_pairs={{0,8},{8,0},{1,9},{9,1},{2,10},{10,2},{3,11},{11,3},{4,12},{12,4},... | collective-permute-start | bytes 1179656 | tf_op jit(solution)/shard_map/ppermute | solution.py:244

commit v8 on v6

--- a/solution.py
+++ b/solution.py
@@ -139,8 +139,8 @@
             turned = pltpu.roll(middle, 64, 1)
             even = jnp.where(lane < 64, middle[top], turned[bottom])
             odd = jnp.where(lane < 64, turned[top], middle[bottom])
-            out_ref[(2 * q) * Y + y] = jnp.concatenate([left, even], 0).astype(jnp.bfloat16)
-            out_ref[(2 * q + 1) * Y + y] = jnp.concatenate([right, odd], 0).astype(jnp.bfloat16)
+            out_ref[y * X + 2 * q] = jnp.concatenate([left, even], 0).astype(jnp.bfloat16)
+            out_ref[y * X + 2 * q + 1] = jnp.concatenate([right, odd], 0).astype(jnp.bfloat16)
 
 
 def exchange_rows(d_own, d_other, b_own, b_other):
@@ -240,7 +240,7 @@
     d_own, b_own, b_other = lax.optimization_barrier((d_own, b_own, b_other))
     d_other = lax.ppermute(d_own, "c", swap)
     parts = exchange_rows(d_own, d_other, *bring(b_own, b_other))
-    parts = lax.all_to_all(parts, ("x", "y"), 0, 0, tiled=True)
+    parts = lax.all_to_all(parts, ("y", "x"), 0, 0, tiled=True)
     parts = lax.all_to_all(sum_xy(parts), ("z", "c"), 0, 0, tiled=True)
     total_ri = three_center.shape[0] * Z * X * C * Y
     return sum_z(parts, 1.0 / math.sqrt(total_ri * A)).T

time: 83 us -> 83.7 us (level)
  blocking collectives: 45.8 us -> 46.7 us
    all_to_all x1, blocking collectives: 19.5 us -> 21.6 us  [per_device(): parts = lax.all_to_all(parts, ('y', 'x'), 0, 0, tiled=True)]
    all_to_all x1, blocking collectives: 26.3 us -> 25.1 us  [per_device(): parts = lax.all_to_all(sum_xy(parts), ('z', 'c'), 0, 0, tiled=True)]
where the time goes in v8:
time: 83.7 us; the launch traced here: 83.3 us
  blocking collectives  46.7 us (56%)
  starting transfers between devices  21.4 us (26%)
  Pallas kernels  10.8 us (13%)
  waiting for transfers between devices  4.27 us (5%)
    all_to_all x1, blocking collectives, per_device(): parts = lax.all_to_all(sum_xy(parts), ('z', 'c'), 0, 0, tiled=True)  25.1 us
    all_to_all x1, blocking collectives, per_device(): parts = lax.all_to_all(parts, ('y', 'x'), 0, 0, tiled=True)  21.6 us
    ppermute x1, starting transfers between devices, per_device(): b_other = lax.ppermute(b_own, 'c', swap)  8.24 us
    all_to_all x1, starting transfers between devices, per_device(): d_own = settle(lax.all_to_all(mine, 'y', 0, 0, tiled=True))  7.65 us
    ppermute x1, starting transfers between devices, per_device(): d_other = lax.ppermute(d_own, 'c', swap)  5.55 us
    pallas_call x1, Pallas kernels, exchange_rows(): pl.pallas_call(functools.partial(exchange_kernel, count), in_specs=[VMEM,...  4.23 us
    ppermute x1, waiting for transfers between devices, per_device(): b_other = lax.ppermute(b_own, 'c', swap)  3.71 us
    pallas_call x1, Pallas kernels, mask_and_order(): pl.pallas_call(mask_kernel, grid=(count,), in_specs=[SMEM, spec], out_spe...  1.94 us
  transfers between devices with their start and end apart: 3, of which 2 were waited for; matrix products, arithmetic and copies ran while one was open for 0% of the time, Pallas kernels for 5%

profile of v8, /device:TPU:1, one launch (start us, length us, event | category | flops | bytes accessed | tf_op | source)
XLA Modules:
  0.0 83.3 jit_solution(13977915356916705164)
XLA Ops:
  0.0 1.8 %pack.1 = bf16[8,96,256]{2,1,0:T(8,128)(2,1)} custom-call(s32[6,6]{1,0:T(8,128)} %d_pattern.1, bf16[96,768]{1,0:T(8,128)(2,1)} %density.1), custom_call_target="tpu_custom_call" | custom-call | tf_op jit(solution)/shard_map/pack/pallas_call | solution.py:176
  1.8 7.7 %all-to-all-start = ((bf16[8,96,256]{2,1,0:T(8,128)(2,1)}), bf16[8,96,256]{2,1,0:T(8,128)(2,1)S(1)}, u32[]{:S(2)}, u32[]{:S(2)}) async-start(bf16[8,96,256]{2,1,0:T(8,128)(2,1)} %pack.1), calls=%async_computation | async-start | bytes 786432 | tf_op jit(solution)/shard_map/all_to_all | solution.py:239
  9.4 1.9 %mask.1.refs_0_ = bf16[2,48,16,768]{3,2,1,0:T(8,128)(2,1)S(1)} custom-call(s32[6,2,6]{2,1,0:T(2,128)} %bitcast.4, bf16[2,48,16,768]{3,2,1,0:T(8,128)(2,1)} %bitcast.3), custom_call_target="tpu_custom_call" | custom-call | flops 99999997952 | tf_op jit(solution)/shard_map/mask/pallas_call | solution.py:55
  11.4 8.2 %collective-permute-start = (bf16[2,48,16,768]{3,2,1,0:T(8,128)(2,1)S(1)}, bf16[2,48,16,768]{3,2,1,0:T(8,128)(2,1)}, u32[]{:S(2)}, u32[]{:S(2)}) collective-permute-start(bf16[2,48,16,768]{3,2,1,0:T(8,128)(2,1)S(1)} %mask.1.refs_0_), channel_id=1, source_target_pairs={{0,8},{8,0},{1,9},{9,1},{2,10},{10,2},{3,11},{11,3},{4,12},{12,4},... | collective-permute-start | bytes 7077896 | tf_op jit(solution)/shard_map/ppermute | solution.py:238
  19.6 0.6 all-to-all-done.in_ref
  20.2 3.7 %collective-permute-done.refs_1_ = bf16[2,48,16,768]{3,2,1,0:T(8,128)(2,1)} collective-permute-done((bf16[2,48,16,768]{3,2,1,0:T(8,128)(2,1)S(1)}, bf16[2,48,16,768]{3,2,1,0:T(8,128)(2,1)}, u32[]{:S(2)}, u32[]{:S(2)}) %collective-permute-start) | collective-permute-done | bytes 2359328 | tf_op jit(solution)/shard_map/ppermute | solution.py:238
  23.9 5.6 %collective-permute-start.1 = (bf16[8,96,256]{2,1,0:T(8,128)(2,1)S(1)}, bf16[8,96,256]{2,1,0:T(8,128)(2,1)S(1)}, u32[]{:S(2)}, u32[]{:S(2)}) collective-permute-start(bf16[8,96,256]{2,1,0:T(8,128)(2,1)S(1)} %settle.1.d_own), channel_id=1, source_target_pairs={{0,8},{8,0},{1,9},{9,1},{2,10},{10,2},{3,11},{11,3},{4,12},{12,4},... | collective-permute-start | bytes 1179656 | tf_op jit(solution)/shard_map/ppermute | solution.py:241
  29.4 1.8 %bring.1 = (bf16[2,48,16,768]{3,2,1,0:T(8,128)(2,1)S(1)}, bf16[2,48,16,768]{3,2,1,0:T(8,128)(2,1)S(1)}) custom-call(bf16[2,48,16,768]{3,2,1,0:T(8,128)(2,1)S(1)} %mask.1.refs_0_, bf16[2,48,16,768]{3,2,1,0:T(8,128)(2,1)} %collective-permute-done.refs_1_), custom_call_target="tpu_custom_call" | custom-call | bytes 9437184 | tf_op jit(solution)/shard_map/bring/pallas_call | solution.py:91
  31.3 0.0 collective-permute-done.1.d_other
  31.3 4.2 %exchange.1 = bf16[32,72,128]{2,1,0:T(8,128)(2,1)S(1)} custom-call(bf16[8,96,256]{2,1,0:T(8,128)(2,1)S(1)} %settle.1.d_own, bf16[8,96,256]{2,1,0:T(8,128)(2,1)S(1)} %collective-permute-done.1.d_other, bf16[2,48,16,768]{3,2,1,0:T(8,128)(2,1)S(1)} %get-tuple-element.17.b_own, bf16[2,48,16,768]{3,2,1,0:T(8,128)(2,1)S(1)} %get-tuple-element.18.b_other), custom_call_target="tpu_custom_call" | custom-call | tf_op jit(solution)/shard_map/exchange/pallas_call | solution.py:148
  35.5 21.6 %all_to_all.15.in_ref = bf16[32,72,128]{2,1,0:T(8,128)(2,1)S(1)} all-to-all(bf16[32,72,128]{2,1,0:T(8,128)(2,1)S(1)} %exchange.1), channel_id=1, replica_groups=mesh['z'=12,'x'=4,'c'=2,'y'=8] {'y','x'}, dimensions={0} | all-to-all | bytes 1179648 | tf_op jit(solution)/shard_map/all_to_all | solution.py:243
  57.2 0.3 sum_xy.1
  57.4 25.1 %all_to_all.16.in_ref = f32[24,4,128]{2,1,0:T(4,128)S(1)} all-to-all(f32[24,4,128]{2,1,0:T(4,128)S(1)} %sum_xy.1), channel_id=1, replica_groups=mesh['z'=12,'x'=4,'c'=2,'y'=8] {'z','c'}, dimensions={0} | all-to-all | bytes 98304 | tf_op jit(solution)/shard_map/all_to_all | solution.py:244
  82.5 0.7 sum_z.1
  (1 shorter events, 0.0 us)
Async XLA Ops:
  1.8 18.4 %all-to-all-start = ((bf16[8,96,256]{2,1,0:T(8,128)(2,1)}), bf16[8,96,256]{2,1,0:T(8,128)(2,1)S(1)}, u32[]{:S(2)}, u32[]{:S(2)}) async-start(bf16[8,96,256]{2,1,0:T(8,128)(2,1)} %pack.1), calls=%async_computation | async-start | bytes 786432 | tf_op jit(solution)/shard_map/all_to_all | solution.py:239
  11.4 12.5 %collective-permute-start = (bf16[2,48,16,768]{3,2,1,0:T(8,128)(2,1)S(1)}, bf16[2,48,16,768]{3,2,1,0:T(8,128)(2,1)}, u32[]{:S(2)}, u32[]{:S(2)}) collective-permute-start(bf16[2,48,16,768]{3,2,1,0:T(8,128)(2,1)S(1)} %mask.1.refs_0_), channel_id=1, source_target_pairs={{0,8},{8,0},{1,9},{9,1},{2,10},{10,2},{3,11},{11,3},{4,12},{12,4},... | collective-permute-start | bytes 7077896 | tf_op jit(solution)/shard_map/ppermute | solution.py:238
  23.9 7.4 %collective-permute-start.1 = (bf16[8,96,256]{2,1,0:T(8,128)(2,1)S(1)}, bf16[8,96,256]{2,1,0:T(8,128)(2,1)S(1)}, u32[]{:S(2)}, u32[]{:S(2)}) collective-permute-start(bf16[8,96,256]{2,1,0:T(8,128)(2,1)S(1)} %settle.1.d_own), channel_id=1, source_target_pairs={{0,8},{8,0},{1,9},{9,1},{2,10},{10,2},{3,11},{11,3},{4,12},{12,4},... | collective-permute-start | bytes 1179656 | tf_op jit(solution)/shard_map/ppermute | solution.py:241

commit v9 on v6

--- a/solution.py
+++ b/solution.py
@@ -194,7 +194,8 @@
         count = part.shape[0] // K
         part = part.reshape(count, K, ROWS)
         pad = jnp.zeros((count, K // 2, 128 - 2 * ROWS), jnp.float32)
-        out_ref[pl.ds(at, count)] = jnp.concatenate([part[:, : K // 2], part[:, K // 2 :], pad], 2)
+        packed = jnp.concatenate([part[:, : K // 2], part[:, K // 2 :], pad], 2)
+        out_ref[pl.ds(at, count)] = packed.astype(jnp.bfloat16)
 
 
 def sum_xy(parts):
@@ -202,7 +203,7 @@
         sum_xy_kernel,
         in_specs=[VMEM],
         out_specs=VMEM,
-        out_shape=pltpu.VMEM((Z * C, K // 2, 128), jnp.float32),
+        out_shape=pltpu.VMEM((Z * C, K // 2, 128), jnp.bfloat16),
         compiler_params=pltpu.CompilerParams(vmem_limit_bytes=8 * MIB),
         name="sum_xy",
     )(vmem(parts))
@@ -211,9 +212,9 @@
 def sum_z_kernel(factor, in_ref, out_ref):
     halves = []
     for c in range(C):
-        total = in_ref[c]
+        total = in_ref[c].astype(jnp.float32)
         for z in range(1, Z):
-            total = total + in_ref[z * C + c]
+            total = total + in_ref[z * C + c].astype(jnp.float32)
         total = jnp.concatenate([total[:, :ROWS], total[:, ROWS : 2 * ROWS]], 0)
         halves.append(total * factor)
     out_ref[...] = jnp.concatenate([halves[g % C][:, g // C * G : (g // C + 1) * G] for g in range(YROWS // G)], 1)

time: 83 us -> 82.7 us (level)
  no operation moved by 1% of the time
where the time goes in v9:
time: 82.7 us; the launch traced here: 82.1 us
  blocking collectives  45.5 us (55%)
  starting transfers between devices  21.4 us (26%)
  Pallas kernels  10.8 us (13%)
  waiting for transfers between devices  4.27 us (5%)
    all_to_all x1, blocking collectives, per_device(): parts = lax.all_to_all(sum_xy(parts), ('z', 'c'), 0, 0, tiled=True)  26 us
    all_to_all x1, blocking collectives, per_device(): parts = lax.all_to_all(parts, ('x', 'y'), 0, 0, tiled=True)  19.5 us
    ppermute x1, starting transfers between devices, per_device(): b_other = lax.ppermute(b_own, 'c', swap)  8.24 us
    all_to_all x1, starting transfers between devices, per_device(): d_own = settle(lax.all_to_all(mine, 'y', 0, 0, tiled=True))  7.65 us
    ppermute x1, starting transfers between devices, per_device(): d_other = lax.ppermute(d_own, 'c', swap)  5.55 us
    pallas_call x1, Pallas kernels, exchange_rows(): pl.pallas_call(functools.partial(exchange_kernel, count), in_specs=[VMEM,...  4.23 us
    ppermute x1, waiting for transfers between devices, per_device(): b_other = lax.ppermute(b_own, 'c', swap)  3.71 us
    pallas_call x1, Pallas kernels, mask_and_order(): pl.pallas_call(mask_kernel, grid=(count,), in_specs=[SMEM, spec], out_spe...  1.94 us
  transfers between devices with their start and end apart: 3, of which 2 were waited for; matrix products, arithmetic and copies ran while one was open for 0% of the time, Pallas kernels for 5%

profile of v9, /device:TPU:1, one launch (start us, length us, event | category | flops | bytes accessed | tf_op | source)
XLA Modules:
  0.0 82.1 jit_solution(3675760721587115991)
XLA Ops:
  0.0 1.8 %pack.1 = bf16[8,96,256]{2,1,0:T(8,128)(2,1)} custom-call(s32[6,6]{1,0:T(8,128)} %d_pattern.1, bf16[96,768]{1,0:T(8,128)(2,1)} %density.1), custom_call_target="tpu_custom_call" | custom-call | tf_op jit(solution)/shard_map/pack/pallas_call | solution.py:176
  1.8 7.7 %all-to-all-start = ((bf16[8,96,256]{2,1,0:T(8,128)(2,1)}), bf16[8,96,256]{2,1,0:T(8,128)(2,1)S(1)}, u32[]{:S(2)}, u32[]{:S(2)}) async-start(bf16[8,96,256]{2,1,0:T(8,128)(2,1)} %pack.1), calls=%async_computation | async-start | bytes 786432 | tf_op jit(solution)/shard_map/all_to_all | solution.py:240
  9.4 1.9 %mask.1.refs_0_ = bf16[2,48,16,768]{3,2,1,0:T(8,128)(2,1)S(1)} custom-call(s32[6,2,6]{2,1,0:T(2,128)} %bitcast.4, bf16[2,48,16,768]{3,2,1,0:T(8,128)(2,1)} %bitcast.3), custom_call_target="tpu_custom_call" | custom-call | flops 99999997952 | tf_op jit(solution)/shard_map/mask/pallas_call | solution.py:55
  11.4 8.2 %collective-permute-start = (bf16[2,48,16,768]{3,2,1,0:T(8,128)(2,1)S(1)}, bf16[2,48,16,768]{3,2,1,0:T(8,128)(2,1)}, u32[]{:S(2)}, u32[]{:S(2)}) collective-permute-start(bf16[2,48,16,768]{3,2,1,0:T(8,128)(2,1)S(1)} %mask.1.refs_0_), channel_id=1, source_target_pairs={{0,8},{8,0},{1,9},{9,1},{2,10},{10,2},{3,11},{11,3},{4,12},{12,4},... | collective-permute-start | bytes 7077896 | tf_op jit(solution)/shard_map/ppermute | solution.py:239
  19.6 0.6 all-to-all-done.in_ref
  20.2 3.7 %collective-permute-done.refs_1_ = bf16[2,48,16,768]{3,2,1,0:T(8,128)(2,1)} collective-permute-done((bf16[2,48,16,768]{3,2,1,0:T(8,128)(2,1)S(1)}, bf16[2,48,16,768]{3,2,1,0:T(8,128)(2,1)}, u32[]{:S(2)}, u32[]{:S(2)}) %collective-permute-start) | collective-permute-done | bytes 2359328 | tf_op jit(solution)/shard_map/ppermute | solution.py:239
  23.9 5.6 %collective-permute-start.1 = (bf16[8,96,256]{2,1,0:T(8,128)(2,1)S(1)}, bf16[8,96,256]{2,1,0:T(8,128)(2,1)S(1)}, u32[]{:S(2)}, u32[]{:S(2)}) collective-permute-start(bf16[8,96,256]{2,1,0:T(8,128)(2,1)S(1)} %settle.1.d_own), channel_id=1, source_target_pairs={{0,8},{8,0},{1,9},{9,1},{2,10},{10,2},{3,11},{11,3},{4,12},{12,4},... | collective-permute-start | bytes 1179656 | tf_op jit(solution)/shard_map/ppermute | solution.py:242
  29.4 1.8 %bring.1 = (bf16[2,48,16,768]{3,2,1,0:T(8,128)(2,1)S(1)}, bf16[2,48,16,768]{3,2,1,0:T(8,128)(2,1)S(1)}) custom-call(bf16[2,48,16,768]{3,2,1,0:T(8,128)(2,1)S(1)} %mask.1.refs_0_, bf16[2,48,16,768]{3,2,1,0:T(8,128)(2,1)} %collective-permute-done.refs_1_), custom_call_target="tpu_custom_call" | custom-call | bytes 9437184 | tf_op jit(solution)/shard_map/bring/pallas_call | solution.py:91
  31.3 0.0 collective-permute-done.1.d_other
  31.3 4.2 %exchange.1 = bf16[32,72,128]{2,1,0:T(8,128)(2,1)S(1)} custom-call(bf16[8,96,256]{2,1,0:T(8,128)(2,1)S(1)} %settle.1.d_own, bf16[8,96,256]{2,1,0:T(8,128)(2,1)S(1)} %collective-permute-done.1.d_other, bf16[2,48,16,768]{3,2,1,0:T(8,128)(2,1)S(1)} %get-tuple-element.17.b_own, bf16[2,48,16,768]{3,2,1,0:T(8,128)(2,1)S(1)} %get-tuple-element.18.b_other), custom_call_target="tpu_custom_call" | custom-call | tf_op jit(solution)/shard_map/exchange/pallas_call | solution.py:148
  35.5 19.5 %all_to_all.15.in_ref = bf16[32,72,128]{2,1,0:T(8,128)(2,1)S(1)} all-to-all(bf16[32,72,128]{2,1,0:T(8,128)(2,1)S(1)} %exchange.1), channel_id=1, replica_groups=mesh['z'=12,'x'=4,'c'=2,'y'=8] {'x','y'}, dimensions={0} | all-to-all | bytes 1179648 | tf_op jit(solution)/shard_map/all_to_all | solution.py:244
  55.1 0.3 sum_xy.1
  55.4 26.0 %all_to_all.16.in_ref = bf16[24,4,128]{2,1,0:T(4,128)(2,1)S(1)} all-to-all(bf16[24,4,128]{2,1,0:T(4,128)(2,1)S(1)} %sum_xy.1), channel_id=1, replica_groups=mesh['z'=12,'x'=4,'c'=2,'y'=8] {'z','c'}, dimensions={0} | all-to-all | bytes 49152 | tf_op jit(solution)/shard_map/all_to_all | solution.py:245
  81.3 0.7 sum_z.1
  (1 shorter events, 0.0 us)
Async XLA Ops:
  1.8 18.4 %all-to-all-start = ((bf16[8,96,256]{2,1,0:T(8,128)(2,1)}), bf16[8,96,256]{2,1,0:T(8,128)(2,1)S(1)}, u32[]{:S(2)}, u32[]{:S(2)}) async-start(bf16[8,96,256]{2,1,0:T(8,128)(2,1)} %pack.1), calls=%async_computation | async-start | bytes 786432 | tf_op jit(solution)/shard_map/all_to_all | solution.py:240
  11.4 12.5 %collective-permute-start = (bf16[2,48,16,768]{3,2,1,0:T(8,128)(2,1)S(1)}, bf16[2,48,16,768]{3,2,1,0:T(8,128)(2,1)}, u32[]{:S(2)}, u32[]{:S(2)}) collective-permute-start(bf16[2,48,16,768]{3,2,1,0:T(8,128)(2,1)S(1)} %mask.1.refs_0_), channel_id=1, source_target_pairs={{0,8},{8,0},{1,9},{9,1},{2,10},{10,2},{3,11},{11,3},{4,12},{12,4},... | collective-permute-start | bytes 7077896 | tf_op jit(solution)/shard_map/ppermute | solution.py:239
  23.9 7.4 %collective-permute-start.1 = (bf16[8,96,256]{2,1,0:T(8,128)(2,1)S(1)}, bf16[8,96,256]{2,1,0:T(8,128)(2,1)S(1)}, u32[]{:S(2)}, u32[]{:S(2)}) collective-permute-start(bf16[8,96,256]{2,1,0:T(8,128)(2,1)S(1)} %settle.1.d_own), channel_id=1, source_target_pairs={{0,8},{8,0},{1,9},{9,1},{2,10},{10,2},{3,11},{11,3},{4,12},{12,4},... | collective-permute-start | bytes 1179656 | tf_op jit(solution)/shard_map/ppermute | solution.py:242

commit v10 on v8

--- a/solution.py
+++ b/solution.py
@@ -77,45 +77,49 @@
     )(part)
 
 
-def bring_kernel(*refs):
-    arrived = refs[-1]
-    count = len(refs) // 2
-    copies = [pltpu.make_async_copy(refs[i], refs[count + i], arrived.at[i]) for i in range(count)]
+def lay(part, h, d):
+    for y in range(Y):
+        for t in range(YROWS // STEP):
+            rb = (y * YROWS + t * STEP) // BS
+            here = slice(y * YROWS + t * STEP, y * YROWS + (t + 1) * STEP)
+            for j in range(SENT // C):
+                col = lax.rem(rb + h * (SENT // C) + j, NB)
+                lanes = pl.ds(pl.multiple_of(col * BS, BS), BS)
+                d[here, lanes] = part[y, t * STEP : (t + 1) * STEP, j * BS : (j + 1) * BS]
+    for rb in range(NB):
+        to = pl.ds(pl.multiple_of(lax.rem(rb + 1 + h, NB) * BS, BS), BS)
+        rows = slice(rb * BS, (rb + 1) * BS)
+        d[to, rows] = d[rows, to].T
+
+
+def bring_kernel(part, *refs):
+    *there, d, arrived = refs
+    count = len(there) // 2
+    copies = [pltpu.make_async_copy(there[i], there[count + i], arrived.at[i]) for i in range(count)]
     for copy in copies:
         copy.start()
+    lay(part, lax.axis_index("c"), d)
     for copy in copies:
         copy.wait()
 
 
-def bring(*there):
+def bring(part, *there):
     return pl.pallas_call(
         bring_kernel,
-        in_specs=[ANY] * len(there),
-        out_specs=[VMEM] * len(there),
-        out_shape=[pltpu.VMEM(x.shape, x.dtype) for x in there],
+        in_specs=[VMEM] + [ANY] * len(there),
+        out_specs=[VMEM] * (len(there) + 1),
+        out_shape=[pltpu.VMEM(x.shape, x.dtype) for x in there] + [pltpu.VMEM((A, A), part.dtype)],
         scratch_shapes=[pltpu.SemaphoreType.DMA((len(there),))],
         cost_estimate=pl.CostEstimate(flops=0, bytes_accessed=sum(x.size * 4 for x in there), transcendentals=0),
         compiler_params=pltpu.CompilerParams(vmem_limit_bytes=MIB),
         name="bring",
-    )(*there)
-
-
-def exchange_kernel(count, d_own, d_other, b_own, b_other, out_ref, d, acc):
+    )(vmem(part), *there)
+
+
+def exchange_kernel(count, d_other, b_own, b_other, d_half, out_ref, d, acc):
+    del d_half
     core = lax.axis_index("c")
-    for h, part in ((core, d_own), (1 - core, d_other)):
-        for y in range(Y):
-            for t in range(YROWS // STEP):
-                rb = (y * YROWS + t * STEP) // BS
-                here = slice(y * YROWS + t * STEP, y * YROWS + (t + 1) * STEP)
-                for j in range(SENT // C):
-                    col = lax.rem(rb + h * (SENT // C) + j, NB)
-                    lanes = pl.ds(pl.multiple_of(col * BS, BS), BS)
-                    d[here, lanes] = part[y, t * STEP : (t + 1) * STEP, j * BS : (j + 1) * BS]
-    for rb in range(NB):
-        for k in range(SENT, NB):
-            cb = (rb + k) % NB
-            rows, cols = slice(rb * BS, (rb + 1) * BS), slice(cb * BS, (cb + 1) * BS)
-            d[rows, cols] = d[cols, rows].T
+    lay(d_other, 1 - core, d)
     lane = lax.broadcasted_iota(jnp.int32, (ROWS // 2, 128), 1)
     top, bottom = slice(0, ROWS // 2), slice(ROWS // 2, ROWS)
     half_rows, halves = Z * G, X // 2
@@ -143,20 +147,18 @@
             out_ref[y * X + 2 * q + 1] = jnp.concatenate([right, odd], 0).astype(jnp.bfloat16)
 
 
-def exchange_rows(d_own, d_other, b_own, b_other):
+def exchange_rows(d_other, b_own, b_other, d):
     count = b_own.shape[0]
     return pl.pallas_call(
         functools.partial(exchange_kernel, count),
         in_specs=[VMEM, VMEM, VMEM, VMEM],
-        out_specs=VMEM,
-        out_shape=pltpu.VMEM((X * Y, PACK, 128), jnp.bfloat16),
-        scratch_shapes=[
-            pltpu.VMEM((A, A), jnp.bfloat16),
-            pltpu.VMEM((Y * ROWS, A), jnp.float32),
-        ],
+        out_specs=[VMEM, VMEM],
+        out_shape=[pltpu.VMEM((X * Y, PACK, 128), jnp.bfloat16), pltpu.VMEM((A, A), jnp.bfloat16)],
+        input_output_aliases={3: 1},
+        scratch_shapes=[pltpu.VMEM((Y * ROWS, A), jnp.float32)],
         compiler_params=pltpu.CompilerParams(vmem_limit_bytes=24 * MIB),
         name="exchange",
-    )(vmem(d_own), vmem(d_other), vmem(b_own), vmem(b_other))
+    )(vmem(d_other), vmem(b_own), vmem(b_other), vmem(d))[0]
 
 
 def pack_kernel(d_pattern, density, out_ref):
@@ -239,7 +241,7 @@
     d_own = settle(lax.all_to_all(mine, "y", 0, 0, tiled=True))
     d_own, b_own, b_other = lax.optimization_barrier((d_own, b_own, b_other))
     d_other = lax.ppermute(d_own, "c", swap)
-    parts = exchange_rows(d_own, d_other, *bring(b_own, b_other))
+    parts = exchange_rows(d_other, *bring(d_own, b_own, b_other))
     parts = lax.all_to_all(parts, ("y", "x"), 0, 0, tiled=True)
     parts = lax.all_to_all(sum_xy(parts), ("z", "c"), 0, 0, tiled=True)
     total_ri = three_center.shape[0] * Z * X * C * Y

time: 83.7 us -> 84 us (level)
  no operation moved by 1% of the time
where the time goes in v10:
time: 84 us; the launch traced here: 83.6 us
  blocking collectives  46.7 us (56%)
  starting transfers between devices  21.4 us (25%)
  Pallas kernels  11.2 us (13%)
  waiting for transfers between devices  4.27 us (5%)
    all_to_all x1, blocking collectives, per_device(): parts = lax.all_to_all(sum_xy(parts), ('z', 'c'), 0, 0, tiled=True)  25.1 us
    all_to_all x1, blocking collectives, per_device(): parts = lax.all_to_all(parts, ('y', 'x'), 0, 0, tiled=True)  21.6 us
    ppermute x1, starting transfers between devices, per_device(): b_other = lax.ppermute(b_own, 'c', swap)  8.24 us
    all_to_all x1, starting transfers between devices, per_device(): d_own = settle(lax.all_to_all(mine, 'y', 0, 0, tiled=True))  7.65 us
    ppermute x1, starting transfers between devices, per_device(): d_other = lax.ppermute(d_own, 'c', swap)  5.55 us
    pallas_call x1, Pallas kernels, exchange_rows(): pl.pallas_call(functools.partial(exchange_kernel, count), in_specs=[VMEM,...  4.53 us
    ppermute x1, waiting for transfers between devices, per_device(): b_other = lax.ppermute(b_own, 'c', swap)  3.71 us
    pallas_call x1, Pallas kernels, mask_and_order(): pl.pallas_call(mask_kernel, grid=(count,), in_specs=[SMEM, spec], out_spe...  1.94 us
  transfers between devices with their start and end apart: 3, of which 2 were waited for; matrix products, arithmetic and copies ran while one was open for 0% of the time, Pallas kernels for 5%

profile of v10, /device:TPU:1, one launch (start us, length us, event | category | flops | bytes accessed | tf_op | source)
XLA Modules:
  0.0 83.6 jit_solution(4192066454375918955)
XLA Ops:
  0.0 1.8 %pack.1 = bf16[8,96,256]{2,1,0:T(8,128)(2,1)} custom-call(s32[6,6]{1,0:T(8,128)} %d_pattern.1, bf16[96,768]{1,0:T(8,128)(2,1)} %density.1), custom_call_target="tpu_custom_call" | custom-call | tf_op jit(solution)/shard_map/pack/pallas_call | solution.py:178
  1.8 7.7 %all-to-all-start = ((bf16[8,96,256]{2,1,0:T(8,128)(2,1)}), bf16[8,96,256]{2,1,0:T(8,128)(2,1)S(1)}, u32[]{:S(2)}, u32[]{:S(2)}) async-start(bf16[8,96,256]{2,1,0:T(8,128)(2,1)} %pack.1), calls=%async_computation | async-start | bytes 786432 | tf_op jit(solution)/shard_map/all_to_all | solution.py:241
  9.4 1.9 %mask.1.refs_0_ = bf16[2,48,16,768]{3,2,1,0:T(8,128)(2,1)S(1)} custom-call(s32[6,2,6]{2,1,0:T(2,128)} %bitcast.4, bf16[2,48,16,768]{3,2,1,0:T(8,128)(2,1)} %bitcast.3), custom_call_target="tpu_custom_call" | custom-call | flops 99999997952 | tf_op jit(solution)/shard_map/mask/pallas_call | solution.py:55
  11.4 8.2 %collective-permute-start = (bf16[2,48,16,768]{3,2,1,0:T(8,128)(2,1)S(1)}, bf16[2,48,16,768]{3,2,1,0:T(8,128)(2,1)}, u32[]{:S(2)}, u32[]{:S(2)}) collective-permute-start(bf16[2,48,16,768]{3,2,1,0:T(8,128)(2,1)S(1)} %mask.1.refs_0_), channel_id=1, source_target_pairs={{0,8},{8,0},{1,9},{9,1},{2,10},{10,2},{3,11},{11,3},{4,12},{12,4},... | collective-permute-start | bytes 7077896 | tf_op jit(solution)/shard_map/ppermute | solution.py:240
  19.6 0.6 all-to-all-done.in_ref
  20.2 3.7 %collective-permute-done.refs_1_ = bf16[2,48,16,768]{3,2,1,0:T(8,128)(2,1)} collective-permute-done((bf16[2,48,16,768]{3,2,1,0:T(8,128)(2,1)S(1)}, bf16[2,48,16,768]{3,2,1,0:T(8,128)(2,1)}, u32[]{:S(2)}, u32[]{:S(2)}) %collective-permute-start) | collective-permute-done | bytes 2359328 | tf_op jit(solution)/shard_map/ppermute | solution.py:240
  23.9 5.6 %collective-permute-start.1 = (bf16[8,96,256]{2,1,0:T(8,128)(2,1)S(1)}, bf16[8,96,256]{2,1,0:T(8,128)(2,1)S(1)}, u32[]{:S(2)}, u32[]{:S(2)}) collective-permute-start(bf16[8,96,256]{2,1,0:T(8,128)(2,1)S(1)} %settle.1.part), channel_id=1, source_target_pairs={{0,8},{8,0},{1,9},{9,1},{2,10},{10,2},{3,11},{11,3},{4,12},{12,4},... | collective-permute-start | bytes 1179656 | tf_op jit(solution)/shard_map/ppermute | solution.py:243
  29.4 1.9 %bring.1 = (bf16[2,48,16,768]{3,2,1,0:T(8,128)(2,1)S(1)}, bf16[2,48,16,768]{3,2,1,0:T(8,128)(2,1)S(1)}, bf16[768,768]{1,0:T(8,128)(2,1)S(1)}) custom-call(bf16[8,96,256]{2,1,0:T(8,128)(2,1)S(1)} %settle.1.part, bf16[2,48,16,768]{3,2,1,0:T(8,128)(2,1)S(1)} %mask.1.refs_0_, bf16[2,48,16,768]{3,2,1,0:T(8,128)(2,1)} %collective-permute-done.refs_1_), custom_call_target="tpu_custom_call" | custom-call | bytes 9437184 | tf_op jit(solution)/shard_map/bring/pallas_call | solution.py:107
  31.4 0.0 collective-permute-done.1.d_other
  31.4 4.5 %exchange.1 = (bf16[32,72,128]{2,1,0:T(8,128)(2,1)S(1)}, bf16[768,768]{1,0:T(8,128)(2,1)S(1)}) custom-call(bf16[8,96,256]{2,1,0:T(8,128)(2,1)S(1)} %collective-permute-done.1.d_other, bf16[2,48,16,768]{3,2,1,0:T(8,128)(2,1)S(1)} %get-tuple-element.19.b_own, bf16[2,48,16,768]{3,2,1,0:T(8,128)(2,1)S(1)} %get-tuple-element.20.b_other, ...), custom_call_target="tpu_custom_call", output_to_operand_aliasing={{1}: (3, {})} | custom-call | tf_op jit(solution)/shard_map/exchange/pallas_call | solution.py:152
  35.9 21.6 %all_to_all.15.in_ref = bf16[32,72,128]{2,1,0:T(8,128)(2,1)S(1)} all-to-all(bf16[32,72,128]{2,1,0:T(8,128)(2,1)S(1)} %get-tuple-element.22), channel_id=1, replica_groups=mesh['z'=12,'x'=4,'c'=2,'y'=8] {'y','x'}, dimensions={0} | all-to-all | bytes 1179648 | tf_op jit(solution)/shard_map/all_to_all | solution.py:245
  57.5 0.3 sum_xy.1
  57.8 25.1 %all_to_all.16.in_ref = f32[24,4,128]{2,1,0:T(4,128)S(1)} all-to-all(f32[24,4,128]{2,1,0:T(4,128)S(1)} %sum_xy.1), channel_id=1, replica_groups=mesh['z'=12,'x'=4,'c'=2,'y'=8] {'z','c'}, dimensions={0} | all-to-all | bytes 98304 | tf_op jit(solution)/shard_map/all_to_all | solution.py:246
  82.9 0.7 sum_z.1
  (1 shorter events, 0.0 us)
Async XLA Ops:
  1.8 18.4 %all-to-all-start = ((bf16[8,96,256]{2,1,0:T(8,128)(2,1)}), bf16[8,96,256]{2,1,0:T(8,128)(2,1)S(1)}, u32[]{:S(2)}, u32[]{:S(2)}) async-start(bf16[8,96,256]{2,1,0:T(8,128)(2,1)} %pack.1), calls=%async_computation | async-start | bytes 786432 | tf_op jit(solution)/shard_map/all_to_all | solution.py:241
  11.4 12.5 %collective-permute-start = (bf16[2,48,16,768]{3,2,1,0:T(8,128)(2,1)S(1)}, bf16[2,48,16,768]{3,2,1,0:T(8,128)(2,1)}, u32[]{:S(2)}, u32[]{:S(2)}) collective-permute-start(bf16[2,48,16,768]{3,2,1,0:T(8,128)(2,1)S(1)} %mask.1.refs_0_), channel_id=1, source_target_pairs={{0,8},{8,0},{1,9},{9,1},{2,10},{10,2},{3,11},{11,3},{4,12},{12,4},... | collective-permute-start | bytes 7077896 | tf_op jit(solution)/shard_map/ppermute | solution.py:240
  23.9 7.5 %collective-permute-start.1 = (bf16[8,96,256]{2,1,0:T(8,128)(2,1)S(1)}, bf16[8,96,256]{2,1,0:T(8,128)(2,1)S(1)}, u32[]{:S(2)}, u32[]{:S(2)}) collective-permute-start(bf16[8,96,256]{2,1,0:T(8,128)(2,1)S(1)} %settle.1.part), channel_id=1, source_target_pairs={{0,8},{8,0},{1,9},{9,1},{2,10},{10,2},{3,11},{11,3},{4,12},{12,4},... | collective-permute-start | bytes 1179656 | tf_op jit(solution)/shard_map/ppermute | solution.py:243
